TPU v7x, 128 devices: a whole 4x4x4 slice. The times are simulated.
128 devices in a mesh: rep: 16 (over z_hi, x, core), tp: 8 (over y, z_lo).
Axes of the slice: x: 4, y: 4, z: 4 (z_hi: 2, z_lo: 2; z = z_hi * 2 + z_lo), core: 2. Of those that a mesh axis runs over, the one named last changes fastest.
Arguments:
- hidden: bfloat16 [16, 4, 5120], P('rep'), may hold values from -6 to 6
- in_gain: bfloat16 [5120], replicated, may hold values from 0.099609375 to 1.8984375
- old_qkv: bfloat16 [5120, 6144], P(None, 'tp'), may hold values from -0.078125 to 0.078125
- old_out: bfloat16 [4096, 5120], P('tp'), may hold values from -0.09375 to 0.09375
- q_gain: bfloat16 [128], replicated, may hold values from 0.099609375 to 1.8984375
- k_gain: bfloat16 [128], replicated, may hold values from 2 to 3
- cache_keys: bfloat16 [16, 8192, 8, 128], P('rep', None, 'tp'), may hold values from -360 to 360
- stored_values: bfloat16 [16, 8192, 8, 128], P('rep', None, 'tp'), may hold values from -6 to 6
- cache_lengths: int32 [16], P('rep'), may hold values from 2048 to 8192, as said below
- new_qkv: bfloat16 [5120, 6144], P(('rep', 'tp')), may hold values from -0.078125 to 0.078125
Outputs:
- attended: bfloat16 [16, 4, 5120], P('rep')
- rollout_qkv: bfloat16 [5120, 6144], P(None, 'tp')
Inputs may be any that keep to these rules, and one draw needn't show every extreme that they name: `cache_lengths`: some sequence has exactly 8192 filled slots in every draw.
All inputs are finite; a program needn't handle non-finite values.
Results may differ from a plain program's by a relative error of at most 0.015.
The roundings to bfloat16 on the way count: a program that leaves them out, or rounds other values in their place, can miss the bound.
Values may be sent and summed in bfloat16 or wider, within the bound.
No kernel may reach another device: no remote copies, remote signals or barrier semaphores. Data moves between devices by JAX's collectives and lax.ppermute only.
A program may use at most 128 MiB of HBM per device.

v0:
```python
import jax
import jax.numpy as jnp
from jax import lax
from jax.sharding import PartitionSpec as P


def rms_norm(values, gain):
    mean_sq = jnp.mean(values * values, axis=-1, keepdims=True)
    return values * lax.rsqrt(mean_sq + 1e-06) * gain


def rotate_pairs(values, positions):
    half_dim = values.shape[-1] // 2
    frequency = 1000000.0 ** (-(jnp.arange(half_dim).astype(jnp.float32) * 2.0 / values.shape[-1]))
    angles = positions[..., None] * frequency
    cosine = jnp.cos(angles)
    sine_part = jnp.sin(angles)
    first_leg = values[..., :half_dim]
    second_leg = values[..., half_dim:]
    return jnp.concatenate(
        [first_leg * cosine - second_leg * sine_part, second_leg * cosine + first_leg * sine_part],
        axis=-1,
    )


def body(
    hidden,
    in_gain,
    old_qkv,
    old_out,
    q_gain,
    k_gain,
    cache_keys,
    stored_values,
    cache_lengths,
    new_qkv,
):
    tall_rows = lax.all_gather(new_qkv, "rep", axis=0, tiled=True)
    mixed_rows = lax.all_to_all(tall_rows, "tp", split_axis=1, concat_axis=0, tiled=True)
    tp_size = lax.axis_size("tp")
    rep_size = lax.axis_size("rep")
    row_count = new_qkv.shape[0]
    rollout_qkv = (
        mixed_rows.reshape(tp_size, rep_size, row_count, -1)
        .transpose(1, 0, 2, 3)
        .reshape(tp_size * rep_size * row_count, -1)
    )
    seq_count, step_count, width = hidden.shape
    head_size = cache_keys.shape[3]
    kv_heads = cache_keys.shape[2]
    slot_count = cache_keys.shape[1]
    query_group = old_out.shape[0] // head_size // kv_heads
    normed = rms_norm(hidden.astype(jnp.float32), in_gain.astype(jnp.float32)).astype(jnp.bfloat16)
    projected_rows = jnp.dot(
        normed.reshape(seq_count * step_count, width), old_qkv, preferred_element_type=jnp.float32
    )
    projected_rows = projected_rows.reshape(
        seq_count, step_count, kv_heads, query_group + 2, head_size
    )
    positions = (cache_lengths[:, None] + jnp.arange(step_count)[None, :]).astype(jnp.float32)
    queries = rotate_pairs(
        rms_norm(projected_rows[:, :, :, :query_group, :], q_gain.astype(jnp.float32)),
        positions[:, :, None, None],
    ).astype(jnp.bfloat16)
    keys_new = rotate_pairs(
        rms_norm(projected_rows[:, :, :, query_group, :], k_gain.astype(jnp.float32)),
        positions[:, :, None],
    ).astype(jnp.bfloat16)
    values_new = projected_rows[:, :, :, query_group + 1, :].astype(jnp.bfloat16)
    scale = 1.0 / jnp.sqrt(jnp.float32(head_size))
    score_old = (
        jnp.einsum("sthgd,sphd->sthgp", queries, cache_keys, preferred_element_type=jnp.float32)
        * scale
    )
    score_new = (
        jnp.einsum("sthgd,suhd->sthgu", queries, keys_new, preferred_element_type=jnp.float32)
        * scale
    )
    slot_ok = jnp.arange(slot_count)[None, :] < cache_lengths[:, None]
    slot_ok = slot_ok[:, None, None, None, :]
    step_ok = jnp.arange(step_count)[None, :] <= jnp.arange(step_count)[:, None]
    step_ok = step_ok[None, :, None, None, :]
    score_old = jnp.where(slot_ok, score_old, -1e30)
    score_new = jnp.where(step_ok, score_new, -1e30)
    top_score = jnp.maximum(
        jnp.max(score_old, axis=-1, keepdims=True), jnp.max(score_new, axis=-1, keepdims=True)
    )
    exp_old = jnp.where(slot_ok, jnp.exp(score_old - top_score), 0.0)
    exp_new = jnp.where(step_ok, jnp.exp(score_new - top_score), 0.0)
    total = jnp.sum(exp_old, axis=-1, keepdims=True) + jnp.sum(exp_new, axis=-1, keepdims=True)
    weight_old = (exp_old / total).astype(jnp.bfloat16)
    weight_new = (exp_new / total).astype(jnp.bfloat16)
    mixed = jnp.einsum(
        "sthgp,sphd->sthgd", weight_old, stored_values, preferred_element_type=jnp.float32
    )
    mixed = mixed + jnp.einsum(
        "sthgu,suhd->sthgd", weight_new, values_new, preferred_element_type=jnp.float32
    )
    heads = mixed.astype(jnp.bfloat16).reshape(
        seq_count * step_count, kv_heads * query_group * head_size
    )
    partial_value = jnp.dot(heads, old_out, preferred_element_type=jnp.float32).reshape(
        seq_count, step_count, width
    )
    attended = lax.psum(partial_value, "tp").astype(jnp.bfloat16)
    return (attended, rollout_qkv)


def solution(mesh):
    in_specs = (
        P("rep", None, None),
        P(),
        P(None, "tp"),
        P("tp", None),
        P(),
        P(),
        P("rep", None, "tp", None),
        P("rep", None, "tp", None),
        P("rep"),
        P(("rep", "tp"), None),
    )
    out_specs = (P("rep", None, None), P(None, "tp"))
    return jax.shard_map(body, mesh=mesh, in_specs=in_specs, out_specs=out_specs, check_vma=False)
```

profile of v0, /device:TPU:0, one launch (start us, length us, event | category | flops | bytes accessed | tf_op | source)
XLA Modules:
  0.0 258.8 jit_solution(2906547456831929637)
XLA Ops:
  7.2 0.7 all-gather.2.cloned.1.call-update
  7.9 75.6 %all-gather.2.cloned.1.call-done = bf16[640,6144]{1,0:T(8,128)(2,1)} async-done(((bf16[40,6144]{1,0:T(8,128)(2,1)}), bf16[640,6144]{1,0:T(8,128)(2,1)}) %all-gather.2.cloned.1.call-update) | async-done | bytes 7864336 | tf_op jit(solution)/shard_map/all_gather | solution.py:38
  83.5 10.6 %copy.35 = bf16[640,6144]{0,1:T(8,128)(2,1)} copy(bf16[640,6144]{1,0:T(8,128)(2,1)} %all-gather.2.cloned.1.call-done) | data formatting | bytes 15728640 | tf_op jit(solution)/shard_map/all_gather | solution.py:38
  94.2 5.0 %all-to-all-start = ((bf16[640,8,768]{0,2,1:T(8,128)(2,1)}), bf16[640,8,768]{0,2,1:T(8,128)(2,1)}, u32[]{:S(2)}, u32[]{:S(2)}) async-start(bf16[640,8,768]{0,2,1:T(8,128)(2,1)} %bitcast.98), calls=%async_computation | async-start | bytes 15728640 | tf_op jit(solution)/shard_map/all_to_all | solution.py:39
  99.9 10.6 %copy.30 = bf16[5120,768]{0,1:T(8,128)(2,1)} copy(bf16[5120,768]{1,0:T(8,128)(2,1)} %param.12) | data formatting | bytes 15728640 | tf_op args[2]
  110.6 0.2 fusion.16
  110.7 5.4 %convolution_bitcast_fusion.1 = f32[1,4,1,6,128]{4,1,3,2,0:T(4,128)S(1)} fusion(bf16[6,128,5120]{2,1,0:T(8,128)(2,1)} %bitcast.99, bf16[1,4,5120]{2,1,0:T(4,128)(2,1)S(1)} %copy-done.1, f32[5120]{0:T(1024)S(1)} %convert_element_type.77, f32[4]{0:T(128)S(1)} %add_rsqrt_fusion.2), kind=kOutput, calls=%fused_computation.8 | convolution fusion | flops 31539200 | bytes 7938064 | tf_op jit(solution)/shard_map/dot_general | solution.py:54
  116.1 0.1 multiply_reduce_fusion
  116.2 0.1 multiply_cosine_fusion.1
  116.6 0.1 multiply_reduce_fusion.1
  116.8 0.1 fusion.45
  116.9 0.2 convolution_multiply_fusion.1
  117.1 0.1 fusion.23
  117.2 0.7 fusion.48
  117.9 0.1 fusion.31
  118.0 0.4 fusion.11
  118.5 0.1 divide_convert_fusion.2
  118.5 0.1 copy.34
  118.7 2.2 fusion.6
  120.9 0.1 fusion.10
  121.0 3.3 %convolution_bitcast_fusion = f32[1,4,5120]{2,1,0:T(4,128)S(1)} fusion(bf16[512,5120]{1,0:T(8,128)(2,1)} %param.13, bf16[1,4,4,128]{3,2,1,0:T(4,128)(2,1)S(1)} %fusion.10), kind=kOutput, calls=%fused_computation.4 | convolution fusion | flops 20971520 | bytes 5328896 | tf_op jit(solution)/shard_map/dot_general | solution.py:102
  124.2 109.8 %psum.7 = bf16[1,4,5120]{2,1,0:T(4,128)(2,1)} all-reduce(f32[1,4,5120]{2,1,0:T(4,128)S(1)} %convolution_bitcast_fusion), channel_id=1, replica_groups=mesh['rep'=16,'tp'=8] {'tp'}, use_global_device_ids=true, to_apply=%region_7.8 | all-reduce | flops 20480 | bytes 122880 | tf_op jit(solution)/shard_map/psum | solution.py:105
  234.0 10.6 %copy.36 = bf16[8,640,768]{2,1,0:T(8,128)(2,1)} copy(bf16[8,640,768]{1,2,0:T(8,128)(2,1)} %bitcast.30) | data formatting | bytes 15728640 | tf_op jit(solution)/shard_map/all_to_all | solution.py:39
  244.7 7.2 %copy.37 = bf16[16,8,40,768]{3,2,1,0:T(8,128)(2,1)} copy(bf16[16,8,40,768]{3,2,0,1:T(8,128)(2,1)} %bitcast.100) | data formatting | bytes 15728640 | tf_op jit(solution)/shard_map/transpose | solution.py:45
  (28 shorter events, 0.5 us)
Async XLA Ops:
  7.2 110.0 %copy-start = (bf16[1,8192,1,128]{3,1,2,0:T(8,128)(2,1)S(1)}, bf16[1,8192,1,128]{3,1,2,0:T(8,128)(2,1)}, u32[]{:S(2)}) copy-start(bf16[1,8192,1,128]{3,1,2,0:T(8,128)(2,1)} %param.16) | copy-start | bytes 6291460
  7.2 76.3 %all-gather.2.cloned.1.call-start = ((), (), s32[]{:S(2)}) async-start(), calls=%async_computation.1 | async-start | bytes 8355840 | tf_op jit(solution)/shard_map/all_gather | solution.py:38
  94.1 5.7 %copy-start.3 = (bf16[128]{0:T(256)(128)(2,1)S(1)}, bf16[128]{0:T(256)(128)(2,1)}, u32[]{:S(2)}) copy-start(bf16[128]{0:T(256)(128)(2,1)} %param.14) | copy-start | bytes 772
  94.1 5.7 %copy-start.4 = (bf16[128]{0:T(256)(128)(2,1)S(1)}, bf16[128]{0:T(256)(128)(2,1)}, u32[]{:S(2)}) copy-start(bf16[128]{0:T(256)(128)(2,1)} %param.15) | copy-start | bytes 772
  94.2 5.7 %copy-start.2 = (bf16[5120]{0:T(1024)(128)(2,1)S(1)}, bf16[5120]{0:T(1024)(128)(2,1)}, u32[]{:S(2)}) copy-start(bf16[5120]{0:T(1024)(128)(2,1)} %param.11) | copy-start | bytes 30724
  94.2 139.9 %all-to-all-start = ((bf16[640,8,768]{0,2,1:T(8,128)(2,1)}), bf16[640,8,768]{0,2,1:T(8,128)(2,1)}, u32[]{:S(2)}, u32[]{:S(2)}) async-start(bf16[640,8,768]{0,2,1:T(8,128)(2,1)} %bitcast.98), calls=%async_computation | async-start | bytes 15728640 | tf_op jit(solution)/shard_map/all_to_all | solution.py:39
  99.9 10.7 %copy-start.1 = (bf16[1,4,5120]{2,1,0:T(4,128)(2,1)S(1)}, bf16[1,4,5120]{2,1,0:T(4,128)(2,1)}, u32[]{:S(2)}) copy-start(bf16[1,4,5120]{2,1,0:T(4,128)(2,1)} %param.10) | copy-start | bytes 122884
Sparse Core Ops, SparseCore 0:
  10.4 73.0 all-gather.1
where the time goes:
time: 260 us; the launch traced here: 259 us
  blocking collectives  110 us (42%)
  waiting for transfers between devices  76.3 us (29%)
  local copies, waits for them, and re-layouts  39.3 us (15%)
  between operations  14.8 us (6%)
  matrix products  11.9 us (5%)
  starting transfers between devices  5.07 us (2%)
    psum x1, blocking collectives, body(): attended = lax.psum(partial_value, 'tp').astype(jnp.bfloat16)  110 us
    all_gather x1, waiting for transfers between devices, body(): tall_rows = lax.all_gather(new_qkv, 'rep', axis=0, tiled=True)  75.6 us
    unnamed x11, local copies, waits for them, and re-layouts  10.7 us
    all_gather x1, local copies, waits for them, and re-layouts, body(): tall_rows = lax.all_gather(new_qkv, 'rep', axis=0, tiled=True)  10.6 us
    all_to_all x1, local copies, waits for them, and re-layouts, body(): lax.all_to_all(tall_rows, 'tp', split_axis=1, concat_axis=0, tiled=True)  10.6 us
    transpose x1, local copies, waits for them, and re-layouts, body(): rollout_qkv = mixed_rows.reshape(tp_size, rep_size, row_count, -1).transp...  7.25 us
    dot_general x1, matrix products, body(): jnp.dot(normed.reshape(seq_count * step_count, width), old_qkv, preferred...  5.36 us
  transfers between devices with their start and end apart: 2, of which 1 were waited for; matrix products, arithmetic and copies ran while one was open for 9% of the time, Pallas kernels for 0%

commit v1 on v0

v1 whole, which is shorter than its diff:
```python
import jax
import jax.numpy as jnp
from jax import lax
from jax.experimental import pallas as pl
from jax.experimental.pallas import tpu as pltpu
from jax.sharding import PartitionSpec as P

BF16 = jnp.bfloat16
F32 = jnp.float32
STEPS = 4
GROUP = 4
HEAD = 128
ROWS = STEPS * GROUP


def rope_tables(cache_lengths):
    half = HEAD // 2
    frequency = 1000000.0 ** (-(jnp.arange(half).astype(F32) * 2.0 / HEAD))
    positions = (cache_lengths[:, None] + jnp.arange(STEPS)[None, :]).astype(F32)
    angles = positions[0, :, None] * frequency
    cosine = jnp.cos(angles)
    sine = jnp.sin(angles)
    return jnp.concatenate([cosine, cosine], axis=-1), jnp.concatenate([-sine, sine], axis=-1)


def attention_kernel(
    length_ref, hidden_ref, in_gain_ref, q_gain_ref, k_gain_ref, cos_ref, sin_ref,
    qkv_hbm, keys_hbm, values_hbm, out_hbm,
    partial_ref,
    qkv, keys, values, wout, scores, sems,
):
    width = qkv.shape[0]
    slots = keys.shape[0]
    qkv_parts, key_parts, value_parts, out_parts = 5, 2, 2, 4
    copies = {}
    sem = 0
    for name, src, dst, parts in (
        ("qkv", qkv_hbm, qkv, qkv_parts),
        ("keys", keys_hbm, keys, key_parts),
        ("values", values_hbm, values, value_parts),
        ("out", out_hbm, wout, out_parts),
    ):
        rows = src.shape[0] // parts
        for part in range(parts):
            span = pl.ds(part * rows, rows)
            copies[name, part] = pltpu.make_async_copy(src.at[span], dst.at[span], sems.at[sem])
            copies[name, part].start()
            sem += 1

    states = hidden_ref[...].astype(F32)
    mean_sq = jnp.mean(states * states, axis=-1, keepdims=True)
    normed = (states * lax.rsqrt(mean_sq + 1e-06) * in_gain_ref[...].astype(F32)).astype(BF16)

    depth = width // qkv_parts
    projected = None
    for part in range(qkv_parts):
        copies["qkv", part].wait()
        term = jnp.dot(
            normed[:, part * depth : (part + 1) * depth],
            qkv[part * depth : (part + 1) * depth, :],
            preferred_element_type=F32,
        )
        projected = term if projected is None else projected + term

    cosine = cos_ref[...]
    sine = sin_ref[...]

    def norm_rotate(block, gain):
        mean = jnp.mean(block * block, axis=-1, keepdims=True)
        block = block * lax.rsqrt(mean + 1e-06) * gain
        swapped = jnp.concatenate([block[:, HEAD // 2 :], block[:, : HEAD // 2]], axis=-1)
        return block * cosine + swapped * sine

    q_gain = q_gain_ref[...].astype(F32)
    queries = jnp.concatenate(
        [norm_rotate(projected[:, j * HEAD : (j + 1) * HEAD], q_gain) for j in range(GROUP)], axis=0
    ).astype(BF16)
    blank = jnp.zeros((ROWS - STEPS, HEAD), F32)
    keys_new = jnp.concatenate(
        [norm_rotate(projected[:, GROUP * HEAD : (GROUP + 1) * HEAD], k_gain_ref[...].astype(F32)), blank],
        axis=0,
    ).astype(BF16)
    values_new = jnp.concatenate([projected[:, (GROUP + 1) * HEAD :], blank], axis=0).astype(BF16)

    length = length_ref[0]
    scale = 1.0 / jnp.sqrt(F32(HEAD))
    contract = (((1,), (1,)), ((), ()))
    new = lax.dot_general(queries, keys_new, contract, preferred_element_type=F32) * scale
    row = lax.broadcasted_iota(jnp.int32, (ROWS, ROWS), 0) % STEPS
    step_ok = lax.broadcasted_iota(jnp.int32, (ROWS, ROWS), 1) <= row
    new = jnp.where(step_ok, new, -1e30)
    top = jnp.max(new, axis=-1, keepdims=True)
    span = slots // key_parts
    for part in range(key_parts):
        copies["keys", part].wait()
        score = lax.dot_general(
            queries, keys[part * span : (part + 1) * span, :], contract, preferred_element_type=F32
        ) * scale
        slot = lax.broadcasted_iota(jnp.int32, (ROWS, span), 1) + part * span
        score = jnp.where(slot < length, score, -1e30)
        scores[:, part * span : (part + 1) * span] = score
        top = jnp.maximum(top, jnp.max(score, axis=-1, keepdims=True))
    exp_new = jnp.where(step_ok, jnp.exp(new - top), 0.0)
    total = jnp.sum(exp_new, axis=-1, keepdims=True)
    for part in range(key_parts):
        exp_old = jnp.exp(scores[:, part * span : (part + 1) * span] - top)
        scores[:, part * span : (part + 1) * span] = exp_old
        total = total + jnp.sum(exp_old, axis=-1, keepdims=True)
    weight_new = (exp_new / total).astype(BF16)
    mixed = jnp.dot(weight_new, values_new, preferred_element_type=F32)
    span = slots // value_parts
    for part in range(value_parts):
        copies["values", part].wait()
        weight = (scores[:, part * span : (part + 1) * span] / total).astype(BF16)
        mixed = mixed + jnp.dot(
            weight, values[part * span : (part + 1) * span, :], preferred_element_type=F32
        )
    heads = jnp.concatenate([mixed[j * STEPS : (j + 1) * STEPS, :] for j in range(GROUP)], axis=-1)
    heads = heads.astype(BF16)
    partial = None
    depth = wout.shape[0] // out_parts
    for part in range(out_parts):
        copies["out", part].wait()
        term = jnp.dot(
            heads[:, part * depth : (part + 1) * depth],
            wout[part * depth : (part + 1) * depth, :],
            preferred_element_type=F32,
        )
        partial = term if partial is None else partial + term
    partial_ref[...] = partial.astype(BF16)


def attention(hidden, in_gain, old_qkv, old_out, q_gain, k_gain, cache_keys, stored_values, cache_lengths):
    width = hidden.shape[-1]
    slots = cache_keys.shape[1]
    cosine, sine = rope_tables(cache_lengths)
    vmem = pl.BlockSpec(memory_space=pltpu.VMEM)
    hbm = pl.BlockSpec(memory_space=pl.ANY)
    return pl.pallas_call(
        attention_kernel,
        out_shape=jax.ShapeDtypeStruct((STEPS, width), BF16),
        in_specs=[pl.BlockSpec(memory_space=pltpu.SMEM)] + [vmem] * 6 + [hbm] * 4,
        out_specs=vmem,
        scratch_shapes=[
            pltpu.VMEM(old_qkv.shape, BF16),
            pltpu.VMEM((slots, HEAD), BF16),
            pltpu.VMEM((slots, HEAD), BF16),
            pltpu.VMEM(old_out.shape, BF16),
            pltpu.VMEM((ROWS, slots), F32),
            pltpu.SemaphoreType.DMA((13,)),
        ],
        compiler_params=pltpu.CompilerParams(vmem_limit_bytes=40 * 1024 * 1024),
        cost_estimate=pl.CostEstimate(flops=120_000_000, bytes_accessed=17_400_000, transcendentals=140_000),
        name="attention",
    )(
        cache_lengths, hidden.reshape(STEPS, width), in_gain.reshape(1, width), q_gain.reshape(1, HEAD),
        k_gain.reshape(1, HEAD), cosine, sine, old_qkv, cache_keys.reshape(slots, HEAD),
        stored_values.reshape(slots, HEAD), old_out,
    )


def place(pieces, shape, previous=None):
    slots = jnp.stack([slot for _, slot, _ in pieces]).astype(jnp.int32)
    arrays = [array for array, _, _ in pieces]
    starts = [start for _, _, start in pieces]
    count = len(arrays)

    def kernel(slots_ref, *refs):
        sources, out, sems = refs[:count], refs[-2], refs[-1]
        copies = []
        for i in range(count):
            copy = pltpu.make_async_copy(
                sources[i], out.at[slots_ref[i], pl.ds(starts[i], sources[i].shape[0])], sems.at[i]
            )
            copy.start()
            copies.append(copy)
        for copy in copies:
            copy.wait()

    hbm = pl.BlockSpec(memory_space=pl.ANY)
    operands = [slots] + arrays + ([] if previous is None else [previous])
    size = sum(a.size for a in arrays) * 2
    return pl.pallas_call(
        kernel,
        out_shape=jax.ShapeDtypeStruct(shape, BF16),
        in_specs=[pl.BlockSpec(memory_space=pltpu.SMEM)] + [hbm] * (len(operands) - 1),
        out_specs=hbm,
        scratch_shapes=[pltpu.SemaphoreType.DMA((count,))],
        input_output_aliases={} if previous is None else {len(operands) - 1: 0},
        cost_estimate=pl.CostEstimate(flops=0, bytes_accessed=2 * size, transcendentals=0),
        name="place",
    )(*operands)


def reshard(new_qkv):
    rows, columns = new_qkv.shape
    tp = lax.axis_size("tp")
    rep = lax.axis_size("rep")
    me = lax.axis_index("rep")
    z, x, core = me // 8, me // 2 % 4, me % 2

    def index(z, x, core):
        return (z * 4 + x) * 2 + core

    def send(array, dz=0, dx=0, dc=0):
        pairs = []
        for i in range(rep):
            a, b, c = i // 8, i // 2 % 4, i % 2
            pairs.append((i, index((a + dz) % 2, (b + dx) % 4, (c + dc) % 2)))
        return lax.ppermute(array, "rep", pairs)

    def slot(dz, dx, dc):
        return index((z + dz) % 2, (x + dx) % 4, (core + dc) % 2)

    half = tp // 2
    blocks = new_qkv.reshape(rows, tp, columns // tp).transpose(1, 0, 2)
    own = lax.all_to_all(blocks, "tp", split_axis=0, concat_axis=0, tiled=True)
    left = send(own, dx=1)
    right = send(own, dx=-1)
    other = send(own, dz=1)
    core_own = send(own, dc=1)
    far_a = send(left[:half], dx=1)
    far_b = send(right[half:], dx=-1)
    other_left = send(other, dx=1)
    other_right = send(other, dx=-1)
    core_first = send(jnp.concatenate([left, right, other]), dc=1)
    other_far_a = send(other_left[:half], dx=1)
    other_far_b = send(other_right[half:], dx=-1)
    core_second = send(jnp.concatenate([far_a, far_b, other_left, other_right]), dc=1)
    core_third = send(jnp.concatenate([other_far_a, other_far_b]), dc=1)

    shape = (rep, tp, rows, columns // tp)
    out = place(
        [
            (own, slot(0, 0, 0), 0),
            (core_own, slot(0, 0, 1), 0),
            (left, slot(0, -1, 0), 0),
            (right, slot(0, 1, 0), 0),
            (other, slot(1, 0, 0), 0),
        ],
        shape,
    )
    out = place(
        [
            (core_first[:tp], slot(0, -1, 1), 0),
            (core_first[tp : 2 * tp], slot(0, 1, 1), 0),
            (core_first[2 * tp :], slot(1, 0, 1), 0),
            (far_a, slot(0, 2, 0), 0),
            (far_b, slot(0, 2, 0), half),
            (other_left, slot(1, -1, 0), 0),
            (other_right, slot(1, 1, 0), 0),
        ],
        shape,
        out,
    )
    out = place(
        [
            (core_second[:tp], slot(0, 2, 1), 0),
            (core_second[tp : 2 * tp], slot(1, -1, 1), 0),
            (core_second[2 * tp :], slot(1, 1, 1), 0),
            (other_far_a, slot(1, 2, 0), 0),
            (other_far_b, slot(1, 2, 0), half),
            (core_third, slot(1, 2, 1), 0),
        ],
        shape,
        out,
    )
    return out.reshape(rep * tp * rows, columns // tp)


def body(
    hidden, in_gain, old_qkv, old_out, q_gain, k_gain, cache_keys, stored_values, cache_lengths, new_qkv
):
    rollout_qkv = reshard(new_qkv)
    partial = attention(
        hidden, in_gain, old_qkv, old_out, q_gain, k_gain, cache_keys, stored_values, cache_lengths
    )
    tp = lax.axis_size("tp")
    copies = jnp.broadcast_to(partial[None], (tp,) + partial.shape)
    terms = lax.all_to_all(copies, "tp", split_axis=0, concat_axis=0, tiled=True)
    attended = jnp.sum(terms.astype(F32), axis=0).astype(BF16)
    return attended.reshape(hidden.shape), rollout_qkv


def solution(mesh):
    in_specs = (
        P("rep", None, None),
        P(),
        P(None, "tp"),
        P("tp", None),
        P(),
        P(),
        P("rep", None, "tp", None),
        P("rep", None, "tp", None),
        P("rep"),
        P(("rep", "tp"), None),
    )
    out_specs = (P("rep", None, None), P(None, "tp"))
    return jax.shard_map(body, mesh=mesh, in_specs=in_specs, out_specs=out_specs, check_vma=False)
```

time: 260 us -> 326 us (1.25)
  the two profiles are of different devices: /device:TPU:0 before, /device:TPU:1 now
where the time goes in v1:
time: 326 us; the launch traced here: 325 us
  Pallas kernels  251 us (77%)
  starting transfers between devices  26.3 us (8%)
  waiting for transfers between devices  16.3 us (5%)
  blocking collectives  14.5 us (4%)
  local copies, waits for them, and re-layouts  12 us (4%)
  other arithmetic  3.73 us (1%)
    pallas_call x3, Pallas kernels, place(): pl.pallas_call(kernel, out_shape=jax.ShapeDtypeStruct(shape, BF16), in_sp...  244 us
    ppermute x13, starting transfers between devices, send(): return lax.ppermute(array, 'rep', pairs)  22.9 us
    all_to_all x1, blocking collectives, reshard(): own = lax.all_to_all(blocks, 'tp', split_axis=0, concat_axis=0, tiled=True)  14.5 us
    ppermute x13, waiting for transfers between devices, send(): return lax.ppermute(array, 'rep', pairs)  14 us
    pallas_call x1, Pallas kernels, attention(): pl.pallas_call(attention_kernel, out_shape=jax.ShapeDtypeStruct((STEPS, w...  6.98 us
  transfers between devices with their start and end apart: 14, of which 3 were waited for; matrix products, arithmetic and copies ran while one was open for 4% of the time, Pallas kernels for 54%

profile of v1, /device:TPU:1, one launch (start us, length us, event | category | flops | bytes accessed | tf_op | source)
XLA Modules:
  0.0 325.1 jit_solution(13012000898517164928)
XLA Ops:
  1.7 14.5 %all_to_all.10.refs_0_ = bf16[8,40,768]{2,1,0:T(8,128)(2,1)S(1)} all-to-all(bf16[8,40,768]{2,1,0:T(8,128)(2,1)S(1)} %bitcast.38), channel_id=1, replica_groups=mesh['rep'=16,'tp'=8] {'tp'}, dimensions={0} | all-to-all | bytes 983040 | tf_op jit(solution)/shard_map/all_to_all | solution.py:217
  16.2 3.3 %collective-permute-start.4 = (bf16[8,40,768]{2,1,0:T(8,128)(2,1)S(1)}, bf16[8,40,768]{2,1,0:T(8,128)(2,1)S(1)}, u32[]{:S(2)}, u32[]{:S(2)}) collective-permute-start(bf16[8,40,768]{2,1,0:T(8,128)(2,1)S(1)} %all_to_all.10.refs_0_), channel_id=1, source_target_pairs={{0,64},{8,72},{16,80},{24,88},{32,96},{40,104},{48,112},{56,120},{... | collective-permute-start | bytes 1474568 | tf_op jit(solution)/shard_map/ppermute | solution.py:210
  20.7 1.5 collective-permute-start.2
  22.2 6.7 %collective-permute-done.4.refs_4_ = bf16[8,40,768]{2,1,0:T(8,128)(2,1)S(1)} collective-permute-done((bf16[8,40,768]{2,1,0:T(8,128)(2,1)S(1)}, bf16[8,40,768]{2,1,0:T(8,128)(2,1)S(1)}, u32[]{:S(2)}, u32[]{:S(2)}) %collective-permute-start.4) | collective-permute-done | bytes 491552 | tf_op jit(solution)/shard_map/ppermute | solution.py:210
  28.9 1.2 collective-permute-start.5
  30.1 1.5 collective-permute-start.6
  31.7 2.7 collective-permute-start.3
  34.4 1.3 pad_maximum_fusion.1
  35.8 4.5 %collective-permute-start.11 = (bf16[24,40,768]{2,1,0:T(8,128)(2,1)}, bf16[24,40,768]{2,1,0:T(8,128)(2,1)}, u32[]{:S(2)}, u32[]{:S(2)}) collective-permute-start(bf16[24,40,768]{2,1,0:T(8,128)(2,1)} %pad_maximum_fusion.1), channel_id=1, source_target_pairs={{0,8},{8,0},{16,24},{24,16},{32,40},{40,32},{48,56},{56,48},{64,72... | collective-permute-start | bytes 4423688 | tf_op jit(solution)/shard_map/ppermute | solution.py:210
  40.3 7.3 %collective-permute-done.1.refs_3_ = bf16[4,40,768]{2,1,0:T(8,128)(2,1)S(1)} collective-permute-done((bf16[4,40,768]{2,1,0:T(8,128)(2,1)S(1)}, bf16[4,40,768]{2,1,0:T(8,128)(2,1)S(1)}, u32[]{:S(2)}, u32[]{:S(2)}) %collective-permute-start.1) | collective-permute-done | bytes 245792 | tf_op jit(solution)/shard_map/ppermute | solution.py:210
  47.7 1.4 pad_maximum_fusion
  49.1 2.6 collective-permute-start.7
  52.7 1.6 copy-done.2
  54.3 7.0 %attention.1 = bf16[4,5120]{1,0:T(4,128)(2,1)S(1)} custom-call(s32[1]{0:T(128)} %copy.24.length_ref, bf16[4,5120]{1,0:T(4,128)(2,1)S(1)} %bitcast.34, bf16[1,5120]{1,0:T(2,128)(2,1)S(1)} %reshape.51.in_gain_ref, bf16[1,128]{1,0:T(2,128)(2,1)S(1)} %bitcast.35, bf16[1,128]{1,0:T(2,128)(2,1)S(1)} %bitcast.36, f32[4,128]{1,0:T(4,128)S(1)} %get-tuple-element.11.cos_ref, ...), custom_call_target="tpu_custom_call" | custom-call | flops 120000000 | bytes 17400000 | tf_op jit(solution)/shard_map/attention/pallas_call | solution.py:139
  62.1 3.4 %all-to-all-start = ((bf16[8,4,5120]{2,1,0:T(4,128)(2,1)}), bf16[8,4,5120]{2,1,0:T(4,128)(2,1)S(1)}, u32[]{:S(2)}, u32[]{:S(2)}) async-start(bf16[8,4,5120]{2,1,0:T(4,128)(2,1)} %broadcast_in_dim.2), calls=%async_computation | async-start | bytes 655360 | tf_op jit(solution)/shard_map/all_to_all | solution.py:280
  65.6 1.2 collective-permute-start.8
  66.8 1.6 collective-permute-start.9
  70.3 2.3 all-to-all-done
  74.1 76.3 %place.3.refs_7_ = bf16[16,8,40,768]{3,2,1,0:T(8,128)(2,1)} custom-call(s32[5]{0:T(128)} %stack.77.slots_ref, bf16[8,40,768]{2,1,0:T(8,128)(2,1)} %copy-done.10, bf16[8,40,768]{2,1,0:T(8,128)(2,1)} %copy-done.16, bf16[8,40,768]{2,1,0:T(8,128)(2,1)} %copy-done.8, bf16[8,40,768]{2,1,0:T(8,128)(2,1)} %copy-done.9, bf16[8,40,768]{2,1,0:T(8,128)(2,1)} %copy-done.11), custom_call_target="tpu_custom_call" | custom-call | bytes 4915200 | tf_op jit(solution)/shard_map/place/pallas_call | solution.py:183
  150.5 1.4 collective-permute-start.10
  152.0 2.5 fusion.1
  154.5 91.2 %place.4.refs_6_ = bf16[16,8,40,768]{3,2,1,0:T(8,128)(2,1)} custom-call(s32[7]{0:T(128)} %stack.71.slots_ref, bf16[8,40,768]{2,1,0:T(8,128)(2,1)} %get-tuple-element.4.refs_0_, bf16[8,40,768]{2,1,0:T(8,128)(2,1)} %get-tuple-element.3.refs_1_, bf16[8,40,768]{2,1,0:T(8,128)(2,1)} %get-tuple-element.2.refs_2_, ...), custom_call_target="tpu_custom_call", output_to_operand_aliasing={{}: (8, {})} | custom-call | bytes 5898240 | tf_op jit(solution)/shard_map/place/pallas_call | solution.py:183
  245.6 2.5 fusion.2
  248.9 76.3 %place.5 = bf16[16,8,40,768]{3,2,1,0:T(8,128)(2,1)} custom-call(s32[6]{0:T(128)} %stack.64.slots_ref, bf16[8,40,768]{2,1,0:T(8,128)(2,1)} %get-tuple-element.7.refs_0_, bf16[8,40,768]{2,1,0:T(8,128)(2,1)} %get-tuple-element.6.refs_1_, bf16[8,40,768]{2,1,0:T(8,128)(2,1)} %get-tuple-element.5.refs_2_, ...), custom_call_target="tpu_custom_call", output_to_operand_aliasing={{}: (7, {})} | custom-call | bytes 4915200 | tf_op jit(solution)/shard_map/place/pallas_call | solution.py:183
  (67 shorter events, 7.9 us)
Async XLA Ops:
  1.7 51.0 %copy-start.1 = (bf16[1,8192,1,128]{3,1,2,0:T(8,128)(2,1)S(1)}, bf16[1,8192,1,128]{3,1,2,0:T(8,128)(2,1)}, u32[]{:S(2)}) copy-start(bf16[1,8192,1,128]{3,1,2,0:T(8,128)(2,1)} %param.16) | copy-start | bytes 6291460
  16.2 36.1 %copy-start.10 = (bf16[8,40,768]{2,1,0:T(8,128)(2,1)}, bf16[8,40,768]{2,1,0:T(8,128)(2,1)S(1)}, u32[]{:S(2)}) copy-start(bf16[8,40,768]{2,1,0:T(8,128)(2,1)S(1)} %all_to_all.10.refs_0_) | copy-start | bytes 1474564
  16.2 12.7 %collective-permute-start.4 = (bf16[8,40,768]{2,1,0:T(8,128)(2,1)S(1)}, bf16[8,40,768]{2,1,0:T(8,128)(2,1)S(1)}, u32[]{:S(2)}, u32[]{:S(2)}) collective-permute-start(bf16[8,40,768]{2,1,0:T(8,128)(2,1)S(1)} %all_to_all.10.refs_0_), channel_id=1, source_target_pairs={{0,64},{8,72},{16,80},{24,88},{32,96},{40,104},{48,112},{56,120},{... | collective-permute-start | bytes 1474568 | tf_op jit(solution)/shard_map/ppermute | solution.py:210
  19.5 12.0 %collective-permute-start = (bf16[8,40,768]{2,1,0:T(8,128)(2,1)S(1)}, bf16[8,40,768]{2,1,0:T(8,128)(2,1)S(1)}, u32[]{:S(2)}, u32[]{:S(2)}) collective-permute-start(bf16[8,40,768]{2,1,0:T(8,128)(2,1)S(1)} %all_to_all.10.refs_0_), channel_id=1, source_target_pairs={{0,16},{8,24},{16,32},{24,40},{32,48},{40,56},{48,0},{56,8},{64,80... | collective-permute-start | bytes 1474568 | tf_op jit(solution)/shard_map/ppermute | solution.py:210
  20.7 10.9 %collective-permute-start.2 = (bf16[8,40,768]{2,1,0:T(8,128)(2,1)S(1)}, bf16[8,40,768]{2,1,0:T(8,128)(2,1)S(1)}, u32[]{:S(2)}, u32[]{:S(2)}) collective-permute-start(bf16[8,40,768]{2,1,0:T(8,128)(2,1)S(1)} %all_to_all.10.refs_0_), channel_id=1, source_target_pairs={{0,48},{8,56},{16,0},{24,8},{32,16},{40,24},{48,32},{56,40},{64,11... | collective-permute-start | bytes 1474568 | tf_op jit(solution)/shard_map/ppermute | solution.py:210
  28.9 6.9 %copy-start.11 = (bf16[8,40,768]{2,1,0:T(8,128)(2,1)}, bf16[8,40,768]{2,1,0:T(8,128)(2,1)S(1)}, u32[]{:S(2)}) copy-start(bf16[8,40,768]{2,1,0:T(8,128)(2,1)S(1)} %collective-permute-done.4.refs_4_) | copy-start | bytes 1474564
  28.9 18.7 %collective-permute-start.5 = (bf16[8,40,768]{2,1,0:T(8,128)(2,1)S(1)}, bf16[8,40,768]{2,1,0:T(8,128)(2,1)S(1)}, u32[]{:S(2)}, u32[]{:S(2)}) collective-permute-start(bf16[8,40,768]{2,1,0:T(8,128)(2,1)S(1)} %collective-permute-done.4.refs_4_), channel_id=1, source_target_pairs={{0,16},{8,24},{16,32},{24,40},{32,48},{40,56},{48,0},{56,8},{64,80... | collective-permute-start | bytes 1474568 | tf_op jit(solution)/shard_map/ppermute | solution.py:210
  30.1 17.5 %collective-permute-start.6 = (bf16[8,40,768]{2,1,0:T(8,128)(2,1)S(1)}, bf16[8,40,768]{2,1,0:T(8,128)(2,1)S(1)}, u32[]{:S(2)}, u32[]{:S(2)}) collective-permute-start(bf16[8,40,768]{2,1,0:T(8,128)(2,1)S(1)} %collective-permute-done.4.refs_4_), channel_id=1, source_target_pairs={{0,48},{8,56},{16,0},{24,8},{32,16},{40,24},{48,32},{56,40},{64,11... | collective-permute-start | bytes 1474568 | tf_op jit(solution)/shard_map/ppermute | solution.py:210
  31.6 16.0 %collective-permute-start.1 = (bf16[4,40,768]{2,1,0:T(8,128)(2,1)S(1)}, bf16[4,40,768]{2,1,0:T(8,128)(2,1)S(1)}, u32[]{:S(2)}, u32[]{:S(2)}) collective-permute-start(bf16[4,40,768]{2,1,0:T(8,128)(2,1)S(1)} %slice.40), channel_id=1, source_target_pairs={{0,16},{8,24},{16,32},{24,40},{32,48},{40,56},{48,0},{56,8},{64,80... | collective-permute-start | bytes 737288 | tf_op jit(solution)/shard_map/ppermute | solution.py:210
  31.7 15.9 %collective-permute-start.3 = (bf16[4,40,768]{2,1,0:T(8,128)(2,1)S(1)}, bf16[4,40,768]{2,1,0:T(8,128)(2,1)S(1)}, u32[]{:S(2)}, u32[]{:S(2)}) collective-permute-start(bf16[4,40,768]{2,1,0:T(8,128)(2,1)S(1)} %slice.41), channel_id=1, source_target_pairs={{0,48},{8,56},{16,0},{24,8},{32,16},{40,24},{48,32},{56,40},{64,11... | collective-permute-start | bytes 737288 | tf_op jit(solution)/shard_map/ppermute | solution.py:210
  34.4 18.2 %copy-start = (bf16[512,5120]{1,0:T(8,128)(2,1)S(1)}, bf16[512,5120]{1,0:T(8,128)(2,1)}, u32[]{:S(2)}) copy-start(bf16[512,5120]{1,0:T(8,128)(2,1)} %out_hbm.1) | copy-start | bytes 15728644
  35.8 16.8 %copy-start.18 = (bf16[5120]{0:T(1024)(128)(2,1)S(1)}, bf16[5120]{0:T(1024)(128)(2,1)}, u32[]{:S(2)}) copy-start(bf16[5120]{0:T(1024)(128)(2,1)} %param.11) | copy-start | bytes 30724
  35.8 16.9 %copy-start.3 = (bf16[1,4,5120]{2,1,0:T(4,128)(2,1)S(1)}, bf16[1,4,5120]{2,1,0:T(4,128)(2,1)}, u32[]{:S(2)}) copy-start(bf16[1,4,5120]{2,1,0:T(4,128)(2,1)} %param.10) | copy-start | bytes 122884
  35.8 16.9 %copy-start.4 = (bf16[128]{0:T(256)(128)(2,1)S(1)}, bf16[128]{0:T(256)(128)(2,1)}, u32[]{:S(2)}) copy-start(bf16[128]{0:T(256)(128)(2,1)} %param.14) | copy-start | bytes 772
  35.8 16.9 %copy-start.5 = (bf16[128]{0:T(256)(128)(2,1)S(1)}, bf16[128]{0:T(256)(128)(2,1)}, u32[]{:S(2)}) copy-start(bf16[128]{0:T(256)(128)(2,1)} %param.15) | copy-start | bytes 772
  35.8 116.2 %collective-permute-start.11 = (bf16[24,40,768]{2,1,0:T(8,128)(2,1)}, bf16[24,40,768]{2,1,0:T(8,128)(2,1)}, u32[]{:S(2)}, u32[]{:S(2)}) collective-permute-start(bf16[24,40,768]{2,1,0:T(8,128)(2,1)} %pad_maximum_fusion.1), channel_id=1, source_target_pairs={{0,8},{8,0},{16,24},{24,16},{32,40},{40,32},{48,56},{56,48},{64,72... | collective-permute-start | bytes 4423688 | tf_op jit(solution)/shard_map/ppermute | solution.py:210
  47.6 17.9 %copy-start.6 = (bf16[8,40,768]{2,1,0:T(8,128)(2,1)}, bf16[8,40,768]{2,1,0:T(8,128)(2,1)S(1)}, u32[]{:S(2)}) copy-start(bf16[8,40,768]{2,1,0:T(8,128)(2,1)S(1)} %collective-permute-done.5.refs_5_) | copy-start | bytes 1474564
  47.6 19.2 %copy-start.7 = (bf16[8,40,768]{2,1,0:T(8,128)(2,1)}, bf16[8,40,768]{2,1,0:T(8,128)(2,1)S(1)}, u32[]{:S(2)}) copy-start(bf16[8,40,768]{2,1,0:T(8,128)(2,1)S(1)} %collective-permute-done.6.refs_6_) | copy-start | bytes 1474564
  49.1 196.5 %collective-permute-start.7 = (bf16[24,40,768]{2,1,0:T(8,128)(2,1)}, bf16[24,40,768]{2,1,0:T(8,128)(2,1)}, u32[]{:S(2)}, u32[]{:S(2)}) collective-permute-start(bf16[24,40,768]{2,1,0:T(8,128)(2,1)} %pad_maximum_fusion), channel_id=1, source_target_pairs={{0,8},{8,0},{16,24},{24,16},{32,40},{40,32},{48,56},{56,48},{64,72... | collective-permute-start | bytes 4423688 | tf_op jit(solution)/shard_map/ppermute | solution.py:210
  52.4 21.0 %collective-permute-start.12 = (bf16[8,40,768]{2,1,0:T(8,128)(2,1)S(1)}, bf16[8,40,768]{2,1,0:T(8,128)(2,1)S(1)}, u32[]{:S(2)}, u32[]{:S(2)}) collective-permute-start(bf16[8,40,768]{2,1,0:T(8,128)(2,1)S(1)} %all_to_all.10.refs_0_), channel_id=1, source_target_pairs={{0,8},{8,0},{16,24},{24,16},{32,40},{40,32},{48,56},{56,48},{64,72... | collective-permute-start | bytes 1474568 | tf_op jit(solution)/shard_map/ppermute | solution.py:210
  62.1 10.5 %all-to-all-start = ((bf16[8,4,5120]{2,1,0:T(4,128)(2,1)}), bf16[8,4,5120]{2,1,0:T(4,128)(2,1)S(1)}, u32[]{:S(2)}, u32[]{:S(2)}) async-start(bf16[8,4,5120]{2,1,0:T(4,128)(2,1)} %broadcast_in_dim.2), calls=%async_computation | async-start | bytes 655360 | tf_op jit(solution)/shard_map/all_to_all | solution.py:280
  65.6 84.8 %collective-permute-start.8 = (bf16[4,40,768]{2,1,0:T(8,128)(2,1)S(1)}, bf16[4,40,768]{2,1,0:T(8,128)(2,1)S(1)}, u32[]{:S(2)}, u32[]{:S(2)}) collective-permute-start(bf16[4,40,768]{2,1,0:T(8,128)(2,1)S(1)} %slice.45), channel_id=1, source_target_pairs={{0,16},{8,24},{16,32},{24,40},{32,48},{40,56},{48,0},{56,8},{64,80... | collective-permute-start | bytes 737288 | tf_op jit(solution)/shard_map/ppermute | solution.py:210
  66.8 83.6 %collective-permute-start.9 = (bf16[4,40,768]{2,1,0:T(8,128)(2,1)S(1)}, bf16[4,40,768]{2,1,0:T(8,128)(2,1)S(1)}, u32[]{:S(2)}, u32[]{:S(2)}) collective-permute-start(bf16[4,40,768]{2,1,0:T(8,128)(2,1)S(1)} %slice.46), channel_id=1, source_target_pairs={{0,48},{8,56},{16,0},{24,8},{32,16},{40,24},{48,32},{56,40},{64,11... | collective-permute-start | bytes 737288 | tf_op jit(solution)/shard_map/ppermute | solution.py:210
  150.5 97.6 %collective-permute-start.10 = (bf16[8,40,768]{2,1,0:T(8,128)(2,1)S(1)}, bf16[8,40,768]{2,1,0:T(8,128)(2,1)S(1)}, u32[]{:S(2)}, u32[]{:S(2)}) collective-permute-start(bf16[8,40,768]{2,1,0:T(8,128)(2,1)S(1)} %pad_maximum_fusion.2), channel_id=1, source_target_pairs={{0,8},{8,0},{16,24},{24,16},{32,40},{40,32},{48,56},{56,48},{64,72... | collective-permute-start | bytes 1474568 | tf_op jit(solution)/shard_map/ppermute | solution.py:210
  (9 other events, 28.8 us)

commit v2 on v1

v2 whole, which is shorter than its diff:
```python
import jax
import jax.numpy as jnp
from jax import lax
from jax.experimental import pallas as pl
from jax.experimental.pallas import tpu as pltpu
from jax.sharding import PartitionSpec as P

BF16 = jnp.bfloat16
F32 = jnp.float32
STEPS = 4
GROUP = 4
HEAD = 128
ROWS = STEPS * GROUP
REP = ("z_hi", "x", "core")
TP = "tp"


def rope_tables(cache_lengths):
    half = HEAD // 2
    frequency = 1000000.0 ** (-(jnp.arange(half).astype(F32) * 2.0 / HEAD))
    positions = (cache_lengths[:, None] + jnp.arange(STEPS)[None, :]).astype(F32)
    angles = positions[0, :, None] * frequency
    cosine = jnp.cos(angles)
    sine = jnp.sin(angles)
    return jnp.concatenate([cosine, cosine], axis=-1), jnp.concatenate([-sine, sine], axis=-1)


def attention_kernel(
    length_ref, cos_ref, sin_ref,
    hidden_hbm, in_gain_hbm, q_gain_hbm, k_gain_hbm, qkv_hbm, keys_hbm, values_hbm, out_hbm,
    partial_ref,
    hidden, in_gain, q_gain, k_gain, qkv, keys, values, wout, scores, sems,
):
    width = qkv.shape[0]
    slots = keys.shape[0]
    qkv_parts, key_parts, value_parts, out_parts = 5, 2, 2, 4
    copies = {}
    sem = 0
    for name, src, dst, parts in (
        ("hidden", hidden_hbm, hidden, 1),
        ("in_gain", in_gain_hbm, in_gain, 1),
        ("q_gain", q_gain_hbm, q_gain, 1),
        ("k_gain", k_gain_hbm, k_gain, 1),
        ("qkv", qkv_hbm, qkv, qkv_parts),
        ("keys", keys_hbm, keys, key_parts),
        ("values", values_hbm, values, value_parts),
        ("out", out_hbm, wout, out_parts),
    ):
        rows = src.shape[0] // parts
        for part in range(parts):
            if parts > 1:
                span = pl.ds(part * rows, rows)
                copies[name, part] = pltpu.make_async_copy(src.at[span], dst.at[span], sems.at[sem])
            else:
                copies[name, part] = pltpu.make_async_copy(src, dst, sems.at[sem])
            copies[name, part].start()
            sem += 1

    for name in ("hidden", "in_gain", "q_gain", "k_gain"):
        copies[name, 0].wait()
    states = hidden[...].astype(F32)
    mean_sq = jnp.mean(states * states, axis=-1, keepdims=True)
    normed = (states * lax.rsqrt(mean_sq + 1e-06) * in_gain[...].astype(F32).reshape(1, width)).astype(BF16)

    depth = width // qkv_parts
    projected = None
    for part in range(qkv_parts):
        copies["qkv", part].wait()
        term = jnp.dot(
            normed[:, part * depth : (part + 1) * depth],
            qkv[part * depth : (part + 1) * depth, :],
            preferred_element_type=F32,
        )
        projected = term if projected is None else projected + term

    cosine = cos_ref[...]
    sine = sin_ref[...]

    def norm_rotate(block, gain):
        mean = jnp.mean(block * block, axis=-1, keepdims=True)
        block = block * lax.rsqrt(mean + 1e-06) * gain
        swapped = jnp.concatenate([block[:, HEAD // 2 :], block[:, : HEAD // 2]], axis=-1)
        return block * cosine + swapped * sine

    q_scale = q_gain[...].astype(F32).reshape(1, HEAD)
    k_scale = k_gain[...].astype(F32).reshape(1, HEAD)
    queries = jnp.concatenate(
        [norm_rotate(projected[:, j * HEAD : (j + 1) * HEAD], q_scale) for j in range(GROUP)], axis=0
    ).astype(BF16)
    blank = jnp.zeros((ROWS - STEPS, HEAD), F32)
    keys_new = jnp.concatenate(
        [norm_rotate(projected[:, GROUP * HEAD : (GROUP + 1) * HEAD], k_scale), blank],
        axis=0,
    ).astype(BF16)
    values_new = jnp.concatenate([projected[:, (GROUP + 1) * HEAD :], blank], axis=0).astype(BF16)

    length = length_ref[0]
    scale = 1.0 / jnp.sqrt(F32(HEAD))
    contract = (((1,), (1,)), ((), ()))
    new = lax.dot_general(queries, keys_new, contract, preferred_element_type=F32) * scale
    row = lax.broadcasted_iota(jnp.int32, (ROWS, ROWS), 0) % STEPS
    step_ok = lax.broadcasted_iota(jnp.int32, (ROWS, ROWS), 1) <= row
    new = jnp.where(step_ok, new, -1e30)
    top = jnp.max(new, axis=-1, keepdims=True)
    span = slots // key_parts
    for part in range(key_parts):
        copies["keys", part].wait()
        score = lax.dot_general(
            queries, keys[part * span : (part + 1) * span, :], contract, preferred_element_type=F32
        ) * scale
        slot = lax.broadcasted_iota(jnp.int32, (ROWS, span), 1) + part * span
        score = jnp.where(slot < length, score, -1e30)
        scores[:, part * span : (part + 1) * span] = score
        top = jnp.maximum(top, jnp.max(score, axis=-1, keepdims=True))
    exp_new = jnp.where(step_ok, jnp.exp(new - top), 0.0)
    total = jnp.sum(exp_new, axis=-1, keepdims=True)
    for part in range(key_parts):
        exp_old = jnp.exp(scores[:, part * span : (part + 1) * span] - top)
        scores[:, part * span : (part + 1) * span] = exp_old
        total = total + jnp.sum(exp_old, axis=-1, keepdims=True)
    weight_new = (exp_new / total).astype(BF16)
    mixed = jnp.dot(weight_new, values_new, preferred_element_type=F32)
    span = slots // value_parts
    for part in range(value_parts):
        copies["values", part].wait()
        weight = (scores[:, part * span : (part + 1) * span] / total).astype(BF16)
        mixed = mixed + jnp.dot(
            weight, values[part * span : (part + 1) * span, :], preferred_element_type=F32
        )
    heads = jnp.concatenate([mixed[j * STEPS : (j + 1) * STEPS, :] for j in range(GROUP)], axis=-1)
    heads = heads.astype(BF16)
    partial = None
    depth = wout.shape[0] // out_parts
    for part in range(out_parts):
        copies["out", part].wait()
        term = jnp.dot(
            heads[:, part * depth : (part + 1) * depth],
            wout[part * depth : (part + 1) * depth, :],
            preferred_element_type=F32,
        )
        partial = term if partial is None else partial + term
    for peer in range(partial_ref.shape[0]):
        partial_ref[peer] = partial.astype(BF16)


def attention(hidden, in_gain, old_qkv, old_out, q_gain, k_gain, cache_keys, stored_values, cache_lengths, tp):
    width = hidden.shape[-1]
    slots = cache_keys.shape[1]
    cosine, sine = rope_tables(cache_lengths)
    vmem = pl.BlockSpec(memory_space=pltpu.VMEM)
    hbm = pl.BlockSpec(memory_space=pltpu.HBM)
    return pl.pallas_call(
        attention_kernel,
        out_shape=jax.ShapeDtypeStruct((tp, STEPS, width), BF16),
        in_specs=[pl.BlockSpec(memory_space=pltpu.SMEM)] + [vmem] * 2 + [hbm] * 8,
        out_specs=vmem,
        scratch_shapes=[
            pltpu.VMEM((STEPS, width), BF16),
            pltpu.VMEM(in_gain.shape, BF16),
            pltpu.VMEM(q_gain.shape, BF16),
            pltpu.VMEM(k_gain.shape, BF16),
            pltpu.VMEM(old_qkv.shape, BF16),
            pltpu.VMEM((slots, HEAD), BF16),
            pltpu.VMEM((slots, HEAD), BF16),
            pltpu.VMEM(old_out.shape, BF16),
            pltpu.VMEM((ROWS, slots), F32),
            pltpu.SemaphoreType.DMA((17,)),
        ],
        compiler_params=pltpu.CompilerParams(vmem_limit_bytes=60 * 1024 * 1024),
        cost_estimate=pl.CostEstimate(flops=120_000_000, bytes_accessed=17_400_000, transcendentals=140_000),
        name="attention",
    )(
        cache_lengths, cosine, sine, hidden.reshape(STEPS, width), in_gain, q_gain, k_gain, old_qkv,
        cache_keys.reshape(slots, HEAD),
        stored_values.reshape(slots, HEAD), old_out,
    )


def place(pieces, shape, previous=None):
    slots = jnp.stack([piece[3] for piece in pieces]).astype(jnp.int32)
    arrays = []
    for piece in pieces:
        if all(piece[0] is not array for array in arrays):
            arrays.append(piece[0])
    which = [next(i for i, array in enumerate(arrays) if array is piece[0]) for piece in pieces]
    count = len(arrays)

    def kernel(slots_ref, *refs):
        sources, out, sems = refs[:count], refs[-2], refs[-1]
        copies = []
        for i, (_, first, size, _, start) in enumerate(pieces):
            copy = pltpu.make_async_copy(
                sources[which[i]].at[pl.ds(first, size)],
                out.at[slots_ref[i], pl.ds(start, size)],
                sems.at[i],
            )
            copy.start()
            copies.append(copy)
        for copy in copies:
            copy.wait()

    operands = [slots] + arrays + ([] if previous is None else [previous])
    size = sum(array.size for array in arrays) * 2
    return pl.pallas_call(
        kernel,
        out_shape=jax.ShapeDtypeStruct(shape, BF16),
        in_specs=[pl.BlockSpec(memory_space=pltpu.SMEM)]
        + [pl.BlockSpec(memory_space=pltpu.VMEM)] * count
        + [pl.BlockSpec(memory_space=pl.ANY)] * (previous is not None),
        out_specs=pl.BlockSpec(memory_space=pl.ANY),
        scratch_shapes=[pltpu.SemaphoreType.DMA((len(pieces),))],
        compiler_params=pltpu.CompilerParams(vmem_limit_bytes=16 * 1024 * 1024),
        input_output_aliases={} if previous is None else {len(operands) - 1: 0},
        cost_estimate=pl.CostEstimate(flops=0, bytes_accessed=2 * size, transcendentals=0),
        name="place",
    )(*operands)


def swap(array, axis):
    return lax.ppermute(array, axis, [(0, 1), (1, 0)])


def ring(array):
    pairs = []
    for x in range(4):
        pairs += [(2 * x, (x + 1) % 4 * 2), (2 * x + 1, (x + 3) % 4 * 2 + 1)]
    return lax.ppermute(array, ("x", "core"), pairs)


def body(
    hidden, in_gain, old_qkv, old_out, q_gain, k_gain, cache_keys, stored_values, cache_lengths, new_qkv
):
    rows, columns = new_qkv.shape
    tp = lax.axis_size(TP)
    rep = lax.axis_size(REP)
    z, x, core = lax.axis_index("z_hi"), lax.axis_index("x"), lax.axis_index("core")
    back = 2 * core + 3

    def slot(dz, dx, dc):
        return ((z + dz) % 2 * 4 + (x + dx) % 4) * 2 + (core + dc) % 2

    blocks = new_qkv.reshape(rows, tp, columns // tp).transpose(1, 0, 2)
    own = lax.all_to_all(blocks, TP, split_axis=0, concat_axis=0, tiled=True)
    partial = attention(
        hidden, in_gain, old_qkv, old_out, q_gain, k_gain, cache_keys, stored_values, cache_lengths, tp
    )
    own, partial = lax.optimization_barrier((own, partial))
    shape = (rep, tp, rows, columns // tp)

    other = swap(own, "z_hi")
    core_own = swap(own, "core")
    near = ring(own)
    near_pair = ring(core_own)
    near, partial = lax.optimization_barrier((near, partial))
    terms = lax.all_to_all(partial, TP, split_axis=0, concat_axis=0, tiled=True)
    far = ring(near)
    core_near = swap(near, "core")
    other_near_pair = swap(near_pair, "z_hi")
    core_near_pair = swap(near_pair, "core")
    core_far = swap(far, "core")
    other_near = ring(other)
    core_other = swap(other, "core")
    out = place(
        [
            (own, 0, tp, slot(0, 0, 0), 0),
            (core_own, 0, tp, slot(0, 0, 1), 0),
            (near, 0, tp, slot(0, back, 0), 0),
            (core_near, 0, tp, slot(0, -back, 1), 0),
            (near_pair, 0, tp, slot(0, back, 1), 0),
            (core_near_pair, 0, tp, slot(0, -back, 0), 0),
        ],
        shape,
    )
    out, terms, other_near = lax.optimization_barrier((out, terms, other_near))
    other_far = ring(other_near)
    core_other_near = swap(other_near, "core")
    attended = terms[0].astype(F32)
    for peer in range(1, tp):
        attended = attended + terms[peer].astype(F32)
    attended = attended.astype(BF16)
    out = place(
        [
            (far, 0, tp, slot(0, 2, 0), 0),
            (core_far, 0, tp, slot(0, 2, 1), 0),
            (other, 0, tp, slot(1, 0, 0), 0),
            (core_other, 0, tp, slot(1, 0, 1), 0),
            (other_near, 0, tp, slot(1, back, 0), 0),
            (core_other_near, 0, tp, slot(1, -back, 1), 0),
        ],
        shape,
        out,
    )
    out, attended, other_near_pair, other_far = lax.optimization_barrier((out, attended, other_near_pair, other_far))
    core_other_near_pair = swap(other_near_pair, "core")
    core_other_far = swap(other_far, "core")
    out = place(
        [
            (other_near_pair, 0, tp, slot(1, back, 1), 0),
            (other_far, 0, tp, slot(1, 2, 0), 0),
            (core_other_near_pair, 0, tp, slot(1, -back, 0), 0),
            (core_other_far, 0, tp, slot(1, 2, 1), 0),
        ],
        shape,
        out,
    )
    return attended.reshape(hidden.shape), out.reshape(rep * tp * rows, columns // tp)


def solution(mesh):
    fine = jax.sharding.Mesh(mesh.devices.reshape(2, 4, 2, mesh.shape["tp"]), REP + (TP,))
    in_specs = (
        P(REP, None, None),
        P(),
        P(None, TP),
        P(TP, None),
        P(),
        P(),
        P(REP, None, TP, None),
        P(REP, None, TP, None),
        P(REP),
        P(REP + (TP,), None),
    )
    out_specs = (P(REP, None, None), P(None, TP))
    return jax.shard_map(body, mesh=fine, in_specs=in_specs, out_specs=out_specs, check_vma=False)
```

time: 326 us -> 69 us (0.21)
  Pallas kernels: 251 us -> 16.5 us
  blocking collectives: 14.5 us -> 0 us
  local copies, waits for them, and re-layouts: 12 us -> 2.01 us
  starting transfers between devices: 26.3 us -> 34.4 us
  waiting for transfers between devices: 16.3 us -> 11.7 us
    pallas_call x3, Pallas kernels: 244 us -> 8.01 us  [place(): pl.pallas_call(kernel, out_shape=jax.ShapeDtypeStruct(shape, BF16), in_sp...]
    all_to_all x1 -> x0, blocking collectives: 14.5 us -> none  [reshard(): own = lax.all_to_all(blocks, 'tp', split_axis=0, concat_axis=0, tiled=True)]
    all_to_all x1 -> x2, starting transfers between devices: 3.43 us -> 11.2 us  [the longest x1 6.37 us: body(): own = lax.all_to_all(blocks, TP, split_axis=0, concat_axis=0, tiled=True)]
    slice x6 -> x0, local copies, waits for them, and re-layouts: 5.03 us -> none  [the longest x1 2.49 us: reshard(): core_first[2 * tp:]]
    ppermute x13 -> x15, waiting for transfers between devices: 14 us -> 11.7 us  [the longest x10 8.82 us: swap(): return lax.ppermute(array, axis, [(0, 1), (1, 0)])]
    ppermute x13 -> x15, starting transfers between devices: 22.9 us -> 23.3 us  [the longest x10 14.9 us: swap(): return lax.ppermute(array, axis, [(0, 1), (1, 0)])]
  transfers between devices with their start and end apart: 14 -> 17, of which waited for: 3 -> 5; matrix products, arithmetic and copies ran while one was open for 4% -> 4% of each run, Pallas kernels for 54% -> 21%
where the time goes in v2:
time: 69 us; the launch traced here: 68.5 us
  starting transfers between devices  34.4 us (50%)
  Pallas kernels  16.5 us (24%)
  waiting for transfers between devices  11.7 us (17%)
  other arithmetic  2.5 us (4%)
  local copies, waits for them, and re-layouts  2.01 us (3%)
  between operations  1.37 us (2%)
    ppermute x10, starting transfers between devices, swap(): return lax.ppermute(array, axis, [(0, 1), (1, 0)])  14.9 us
    ppermute x10, waiting for transfers between devices, swap(): return lax.ppermute(array, axis, [(0, 1), (1, 0)])  8.82 us
    pallas_call x1, Pallas kernels, attention(): pl.pallas_call(attention_kernel, out_shape=jax.ShapeDtypeStruct((tp, STEP...  8.51 us
    ppermute x5, starting transfers between devices, ring(): return lax.ppermute(array, ('x', 'core'), pairs)  8.39 us
    pallas_call x3, Pallas kernels, place(): pl.pallas_call(kernel, out_shape=jax.ShapeDtypeStruct(shape, BF16), in_sp...  8.01 us
    all_to_all x1, starting transfers between devices, body(): own = lax.all_to_all(blocks, TP, split_axis=0, concat_axis=0, tiled=True)  6.37 us
    all_to_all x1, starting transfers between devices, body(): terms = lax.all_to_all(partial, TP, split_axis=0, concat_axis=0, tiled=True)  4.79 us
    ppermute x5, waiting for transfers between devices, ring(): return lax.ppermute(array, ('x', 'core'), pairs)  2.84 us
  transfers between devices with their start and end apart: 17, of which 5 were waited for; matrix products, arithmetic and copies ran while one was open for 4% of the time, Pallas kernels for 21%

profile of v2, /device:TPU:1, one launch (start us, length us, event | category | flops | bytes accessed | tf_op | source)
XLA Modules:
  0.0 68.5 jit_solution(1968220406791869922)
XLA Ops:
  0.6 1.8 %copy.17 = bf16[5,8,8,768]{3,2,0,1:T(8,128)(2,1)} copy(bf16[5,8,8,768]{3,2,1,0:T(8,128)(2,1)} %bitcast.35) | data formatting | bytes 983040 | tf_op jit(solution)/shard_map/reshape | solution.py:242
  2.5 6.4 %all-to-all-start = ((bf16[8,40,768]{2,1,0:T(8,128)(2,1)}), bf16[8,40,768]{2,1,0:T(8,128)(2,1)S(1)}, u32[]{:S(2)}, u32[]{:S(2)}) async-start(bf16[8,40,768]{2,1,0:T(8,128)(2,1)} %bitcast.30), calls=%async_computation | async-start | bytes 983040 | tf_op jit(solution)/shard_map/all_to_all | solution.py:243
  10.3 8.5 %attention.1 = bf16[8,4,5120]{2,1,0:T(4,128)(2,1)} custom-call(s32[1]{0:T(128)} %copy.20.length_ref, f32[4,128]{1,0:T(4,128)} %get-tuple-element.27.cos_ref, f32[4,128]{1,0:T(4,128)} %get-tuple-element.28.sin_ref, bf16[4,5120]{1,0:T(4,128)(2,1)} %bitcast.36, bf16[5120]{0:T(1024)(128)(2,1)} %in_gain_hbm.1, bf16[128]{0:T(256)(128)(2,1)} %q_gain_hbm.1, ...), custom_call_target="tpu_custom_call" | custom-call | flops 120000000 | bytes 17400000 | tf_op jit(solution)/shard_map/attention/pallas_call | solution.py:152
  18.8 1.0 %collective-permute-start.5 = (bf16[8,40,768]{2,1,0:T(8,128)(2,1)S(1)}, bf16[8,40,768]{2,1,0:T(8,128)(2,1)S(1)}, u32[]{:S(2)}, u32[]{:S(2)}) collective-permute-start(bf16[8,40,768]{2,1,0:T(8,128)(2,1)S(1)} %all-to-all-done.refs_0_), channel_id=1, source_target_pairs={{0,8},{8,0},{1,9},{9,1},{2,10},{10,2},{3,11},{11,3},{4,12},{12,4},... | collective-permute-start | bytes 1474568 | tf_op jit(solution)/shard_map/ppermute | solution.py:220
  19.9 2.5 %collective-permute-start = (bf16[8,40,768]{2,1,0:T(8,128)(2,1)S(1)}, bf16[8,40,768]{2,1,0:T(8,128)(2,1)S(1)}, u32[]{:S(2)}, u32[]{:S(2)}) collective-permute-start(bf16[8,40,768]{2,1,0:T(8,128)(2,1)S(1)} %all-to-all-done.refs_0_), channel_id=1, source_target_pairs={{0,16},{8,56},{16,32},{24,8},{32,48},{40,24},{48,0},{56,40},{1,17}... | collective-permute-start | bytes 1474568 | tf_op jit(solution)/shard_map/ppermute | solution.py:227
  22.4 1.5 %collective-permute-start.7 = (bf16[8,40,768]{2,1,0:T(8,128)(2,1)S(1)}, bf16[8,40,768]{2,1,0:T(8,128)(2,1)S(1)}, u32[]{:S(2)}, u32[]{:S(2)}) collective-permute-start(bf16[8,40,768]{2,1,0:T(8,128)(2,1)S(1)} %collective-permute-done.5.refs_1_), channel_id=1, source_target_pairs={{0,16},{8,56},{16,32},{24,8},{32,48},{40,24},{48,0},{56,40},{1,17}... | collective-permute-start | bytes 1474568 | tf_op jit(solution)/shard_map/ppermute | solution.py:227
  23.8 3.3 %collective-permute-start.3 = (bf16[8,40,768]{2,1,0:T(8,128)(2,1)S(1)}, bf16[8,40,768]{2,1,0:T(8,128)(2,1)S(1)}, u32[]{:S(2)}, u32[]{:S(2)}) collective-permute-start(bf16[8,40,768]{2,1,0:T(8,128)(2,1)S(1)} %all-to-all-done.refs_0_), channel_id=1, source_target_pairs={{0,64},{64,0},{1,65},{65,1},{2,66},{66,2},{3,67},{67,3},{4,68},{68... | collective-permute-start | bytes 1474568 | tf_op jit(solution)/shard_map/ppermute | solution.py:220
  28.1 1.9 %collective-permute-start.6 = (bf16[8,40,768]{2,1,0:T(8,128)(2,1)S(1)}, bf16[8,40,768]{2,1,0:T(8,128)(2,1)}, u32[]{:S(2)}, u32[]{:S(2)}) collective-permute-start(bf16[8,40,768]{2,1,0:T(8,128)(2,1)S(1)} %collective-permute-done.refs_2_), channel_id=1, source_target_pairs={{0,8},{8,0},{1,9},{9,1},{2,10},{10,2},{3,11},{11,3},{4,12},{12,4},... | collective-permute-start | bytes 1474568 | tf_op jit(solution)/shard_map/ppermute | solution.py:220
  30.0 1.5 %collective-permute-start.1 = (bf16[8,40,768]{2,1,0:T(8,128)(2,1)S(1)}, bf16[8,40,768]{2,1,0:T(8,128)(2,1)S(1)}, u32[]{:S(2)}, u32[]{:S(2)}) collective-permute-start(bf16[8,40,768]{2,1,0:T(8,128)(2,1)S(1)} %collective-permute-done.refs_2_), channel_id=1, source_target_pairs={{0,16},{8,56},{16,32},{24,8},{32,48},{40,24},{48,0},{56,40},{1,17}... | collective-permute-start | bytes 1474568 | tf_op jit(solution)/shard_map/ppermute | solution.py:227
  31.5 1.9 %collective-permute-done.7.refs_4_ = bf16[8,40,768]{2,1,0:T(8,128)(2,1)S(1)} collective-permute-done((bf16[8,40,768]{2,1,0:T(8,128)(2,1)S(1)}, bf16[8,40,768]{2,1,0:T(8,128)(2,1)S(1)}, u32[]{:S(2)}, u32[]{:S(2)}) %collective-permute-start.7) | collective-permute-done | bytes 491552 | tf_op jit(solution)/shard_map/ppermute | solution.py:227
  33.4 1.9 %collective-permute-start.8 = (bf16[8,40,768]{2,1,0:T(8,128)(2,1)S(1)}, bf16[8,40,768]{2,1,0:T(8,128)(2,1)}, u32[]{:S(2)}, u32[]{:S(2)}) collective-permute-start(bf16[8,40,768]{2,1,0:T(8,128)(2,1)S(1)} %collective-permute-done.7.refs_4_), channel_id=1, source_target_pairs={{0,8},{8,0},{1,9},{9,1},{2,10},{10,2},{3,11},{11,3},{4,12},{12,4},... | collective-permute-start | bytes 1474568 | tf_op jit(solution)/shard_map/ppermute | solution.py:220
  35.3 2.9 %collective-permute-done.3.refs_2_ = bf16[8,40,768]{2,1,0:T(8,128)(2,1)S(1)} collective-permute-done((bf16[8,40,768]{2,1,0:T(8,128)(2,1)S(1)}, bf16[8,40,768]{2,1,0:T(8,128)(2,1)S(1)}, u32[]{:S(2)}, u32[]{:S(2)}) %collective-permute-start.3) | collective-permute-done | bytes 491552 | tf_op jit(solution)/shard_map/ppermute | solution.py:220
  39.1 4.8 %all-to-all-start.1 = ((bf16[8,4,5120]{2,1,0:T(4,128)(2,1)}), bf16[8,4,5120]{2,1,0:T(4,128)(2,1)}, u32[]{:S(2)}, u32[]{:S(2)}) async-start(bf16[8,4,5120]{2,1,0:T(4,128)(2,1)} %attention.1), calls=%async_computation.1 | async-start | bytes 655360 | tf_op jit(solution)/shard_map/all_to_all | solution.py:255
  44.0 1.1 %collective-permute-start.4 = (bf16[8,40,768]{2,1,0:T(8,128)(2,1)S(1)}, bf16[8,40,768]{2,1,0:T(8,128)(2,1)}, u32[]{:S(2)}, u32[]{:S(2)}) collective-permute-start(bf16[8,40,768]{2,1,0:T(8,128)(2,1)S(1)} %collective-permute-done.3.refs_2_), channel_id=1, source_target_pairs={{0,8},{8,0},{1,9},{9,1},{2,10},{10,2},{3,11},{11,3},{4,12},{12,4},... | collective-permute-start | bytes 1474568 | tf_op jit(solution)/shard_map/ppermute | solution.py:220
  45.1 3.3 %collective-permute-start.11 = (bf16[8,40,768]{2,1,0:T(8,128)(2,1)S(1)}, bf16[8,40,768]{2,1,0:T(8,128)(2,1)}, u32[]{:S(2)}, u32[]{:S(2)}) collective-permute-start(bf16[8,40,768]{2,1,0:T(8,128)(2,1)S(1)} %collective-permute-done.7.refs_4_), channel_id=1, source_target_pairs={{0,64},{64,0},{1,65},{65,1},{2,66},{66,2},{3,67},{67,3},{4,68},{68... | collective-permute-start | bytes 1474568 | tf_op jit(solution)/shard_map/ppermute | solution.py:220
  48.8 2.8 %place.3.refs_6_ = bf16[16,8,40,768]{3,2,1,0:T(8,128)(2,1)} custom-call(s32[6]{0:T(128)S(1)} %stack.70.slots_ref, bf16[8,40,768]{2,1,0:T(8,128)(2,1)S(1)} %all-to-all-done.refs_0_, bf16[8,40,768]{2,1,0:T(8,128)(2,1)S(1)} %collective-permute-done.5.refs_1_, bf16[8,40,768]{2,1,0:T(8,128)(2,1)S(1)} %collective-permute-done.refs_2_, ...), custom_call_target="tpu_custom_call" | custom-call | bytes 5898240 | tf_op jit(solution)/shard_map/place/pallas_call | solution.py:204
  51.7 1.0 %collective-permute-start.10 = (bf16[8,40,768]{2,1,0:T(8,128)(2,1)S(1)}, bf16[8,40,768]{2,1,0:T(8,128)(2,1)S(1)}, u32[]{:S(2)}, u32[]{:S(2)}) collective-permute-start(bf16[8,40,768]{2,1,0:T(8,128)(2,1)S(1)} %collective-permute-done.9.refs_4_), channel_id=1, source_target_pairs={{0,8},{8,0},{1,9},{9,1},{2,10},{10,2},{3,11},{11,3},{4,12},{12,4},... | collective-permute-start | bytes 1474568 | tf_op jit(solution)/shard_map/ppermute | solution.py:220
  52.7 2.0 %collective-permute-start.12 = (bf16[8,40,768]{2,1,0:T(8,128)(2,1)S(1)}, bf16[8,40,768]{2,1,0:T(8,128)(2,1)S(1)}, u32[]{:S(2)}, u32[]{:S(2)}) collective-permute-start(bf16[8,40,768]{2,1,0:T(8,128)(2,1)S(1)} %collective-permute-done.9.refs_4_), channel_id=1, source_target_pairs={{0,16},{8,56},{16,32},{24,8},{32,48},{40,24},{48,0},{56,40},{1,17}... | collective-permute-start | bytes 1474568 | tf_op jit(solution)/shard_map/ppermute | solution.py:227
  54.7 1.6 %fusion = bf16[4,5120]{1,0:T(4,128)(2,1)} fusion(bf16[8,4,5120]{2,1,0:T(4,128)(2,1)} %all-to-all-done.1), kind=kLoop, calls=%fused_computation.2 | loop fusion | flops 327680 | bytes 368640 | tf_op jit(solution)/shard_map/convert_element_type | solution.py:280
  56.3 2.8 %place.4.refs_4_ = bf16[16,8,40,768]{3,2,1,0:T(8,128)(2,1)} custom-call(s32[6]{0:T(128)S(1)} %stack.63.slots_ref, bf16[8,40,768]{2,1,0:T(8,128)(2,1)S(1)} %collective-permute-done.1.refs_0_, bf16[8,40,768]{2,1,0:T(8,128)(2,1)} %collective-permute-done.2.refs_1_, ...), custom_call_target="tpu_custom_call", output_to_operand_aliasing={{}: (7, {})} | custom-call | bytes 5898240 | tf_op jit(solution)/shard_map/place/pallas_call | solution.py:204
  59.2 3.6 %collective-permute-done.11.refs_0_ = bf16[8,40,768]{2,1,0:T(8,128)(2,1)} collective-permute-done((bf16[8,40,768]{2,1,0:T(8,128)(2,1)S(1)}, bf16[8,40,768]{2,1,0:T(8,128)(2,1)}, u32[]{:S(2)}, u32[]{:S(2)}) %collective-permute-start.11) | collective-permute-done | bytes 491552 | tf_op jit(solution)/shard_map/ppermute | solution.py:220
  62.8 1.0 %collective-permute-start.13 = (bf16[8,40,768]{2,1,0:T(8,128)(2,1)}, bf16[8,40,768]{2,1,0:T(8,128)(2,1)S(1)}, u32[]{:S(2)}, u32[]{:S(2)}) collective-permute-start(bf16[8,40,768]{2,1,0:T(8,128)(2,1)} %collective-permute-done.11.refs_0_), channel_id=1, source_target_pairs={{0,8},{8,0},{1,9},{9,1},{2,10},{10,2},{3,11},{11,3},{4,12},{12,4},... | collective-permute-start | bytes 1474568 | tf_op jit(solution)/shard_map/ppermute | solution.py:220
  63.9 2.3 %collective-permute-done.13.refs_2_ = bf16[8,40,768]{2,1,0:T(8,128)(2,1)S(1)} collective-permute-done((bf16[8,40,768]{2,1,0:T(8,128)(2,1)}, bf16[8,40,768]{2,1,0:T(8,128)(2,1)S(1)}, u32[]{:S(2)}, u32[]{:S(2)}) %collective-permute-start.13) | collective-permute-done | bytes 491552 | tf_op jit(solution)/shard_map/ppermute | solution.py:220
  66.2 2.3 %place.5 = bf16[16,8,40,768]{3,2,1,0:T(8,128)(2,1)} custom-call(s32[4]{0:T(128)S(1)} %pad_add_fusion.slots_ref, bf16[8,40,768]{2,1,0:T(8,128)(2,1)} %collective-permute-done.11.refs_0_, bf16[8,40,768]{2,1,0:T(8,128)(2,1)S(1)} %collective-permute-done.12.refs_1_, ...), custom_call_target="tpu_custom_call", output_to_operand_aliasing={{}: (5, {})} | custom-call | bytes 3932160 | tf_op jit(solution)/shard_map/place/pallas_call | solution.py:204
  (23 shorter events, 3.3 us)
Async XLA Ops:
  2.5 16.4 %all-to-all-start = ((bf16[8,40,768]{2,1,0:T(8,128)(2,1)}), bf16[8,40,768]{2,1,0:T(8,128)(2,1)S(1)}, u32[]{:S(2)}, u32[]{:S(2)}) async-start(bf16[8,40,768]{2,1,0:T(8,128)(2,1)} %bitcast.30), calls=%async_computation | async-start | bytes 983040 | tf_op jit(solution)/shard_map/all_to_all | solution.py:243
  18.8 3.5 %collective-permute-start.5 = (bf16[8,40,768]{2,1,0:T(8,128)(2,1)S(1)}, bf16[8,40,768]{2,1,0:T(8,128)(2,1)S(1)}, u32[]{:S(2)}, u32[]{:S(2)}) collective-permute-start(bf16[8,40,768]{2,1,0:T(8,128)(2,1)S(1)} %all-to-all-done.refs_0_), channel_id=1, source_target_pairs={{0,8},{8,0},{1,9},{9,1},{2,10},{10,2},{3,11},{11,3},{4,12},{12,4},... | collective-permute-start | bytes 1474568 | tf_op jit(solution)/shard_map/ppermute | solution.py:220
  19.9 8.3 %collective-permute-start = (bf16[8,40,768]{2,1,0:T(8,128)(2,1)S(1)}, bf16[8,40,768]{2,1,0:T(8,128)(2,1)S(1)}, u32[]{:S(2)}, u32[]{:S(2)}) collective-permute-start(bf16[8,40,768]{2,1,0:T(8,128)(2,1)S(1)} %all-to-all-done.refs_0_), channel_id=1, source_target_pairs={{0,16},{8,56},{16,32},{24,8},{32,48},{40,24},{48,0},{56,40},{1,17}... | collective-permute-start | bytes 1474568 | tf_op jit(solution)/shard_map/ppermute | solution.py:227
  22.4 11.0 %collective-permute-start.7 = (bf16[8,40,768]{2,1,0:T(8,128)(2,1)S(1)}, bf16[8,40,768]{2,1,0:T(8,128)(2,1)S(1)}, u32[]{:S(2)}, u32[]{:S(2)}) collective-permute-start(bf16[8,40,768]{2,1,0:T(8,128)(2,1)S(1)} %collective-permute-done.5.refs_1_), channel_id=1, source_target_pairs={{0,16},{8,56},{16,32},{24,8},{32,48},{40,24},{48,0},{56,40},{1,17}... | collective-permute-start | bytes 1474568 | tf_op jit(solution)/shard_map/ppermute | solution.py:227
  23.8 14.4 %collective-permute-start.3 = (bf16[8,40,768]{2,1,0:T(8,128)(2,1)S(1)}, bf16[8,40,768]{2,1,0:T(8,128)(2,1)S(1)}, u32[]{:S(2)}, u32[]{:S(2)}) collective-permute-start(bf16[8,40,768]{2,1,0:T(8,128)(2,1)S(1)} %all-to-all-done.refs_0_), channel_id=1, source_target_pairs={{0,64},{64,0},{1,65},{65,1},{2,66},{66,2},{3,67},{67,3},{4,68},{68... | collective-permute-start | bytes 1474568 | tf_op jit(solution)/shard_map/ppermute | solution.py:220
  28.1 17.0 %collective-permute-start.6 = (bf16[8,40,768]{2,1,0:T(8,128)(2,1)S(1)}, bf16[8,40,768]{2,1,0:T(8,128)(2,1)}, u32[]{:S(2)}, u32[]{:S(2)}) collective-permute-start(bf16[8,40,768]{2,1,0:T(8,128)(2,1)S(1)} %collective-permute-done.refs_2_), channel_id=1, source_target_pairs={{0,8},{8,0},{1,9},{9,1},{2,10},{10,2},{3,11},{11,3},{4,12},{12,4},... | collective-permute-start | bytes 1474568 | tf_op jit(solution)/shard_map/ppermute | solution.py:220
  30.0 18.5 %collective-permute-start.1 = (bf16[8,40,768]{2,1,0:T(8,128)(2,1)S(1)}, bf16[8,40,768]{2,1,0:T(8,128)(2,1)S(1)}, u32[]{:S(2)}, u32[]{:S(2)}) collective-permute-start(bf16[8,40,768]{2,1,0:T(8,128)(2,1)S(1)} %collective-permute-done.refs_2_), channel_id=1, source_target_pairs={{0,16},{8,56},{16,32},{24,8},{32,48},{40,24},{48,0},{56,40},{1,17}... | collective-permute-start | bytes 1474568 | tf_op jit(solution)/shard_map/ppermute | solution.py:227
  33.4 15.4 %collective-permute-start.8 = (bf16[8,40,768]{2,1,0:T(8,128)(2,1)S(1)}, bf16[8,40,768]{2,1,0:T(8,128)(2,1)}, u32[]{:S(2)}, u32[]{:S(2)}) collective-permute-start(bf16[8,40,768]{2,1,0:T(8,128)(2,1)S(1)} %collective-permute-done.7.refs_4_), channel_id=1, source_target_pairs={{0,8},{8,0},{1,9},{9,1},{2,10},{10,2},{3,11},{11,3},{4,12},{12,4},... | collective-permute-start | bytes 1474568 | tf_op jit(solution)/shard_map/ppermute | solution.py:220
  38.2 13.5 %collective-permute-start.9 = (bf16[8,40,768]{2,1,0:T(8,128)(2,1)S(1)}, bf16[8,40,768]{2,1,0:T(8,128)(2,1)S(1)}, u32[]{:S(2)}, u32[]{:S(2)}) collective-permute-start(bf16[8,40,768]{2,1,0:T(8,128)(2,1)S(1)} %collective-permute-done.3.refs_2_), channel_id=1, source_target_pairs={{0,16},{8,56},{16,32},{24,8},{32,48},{40,24},{48,0},{56,40},{1,17}... | collective-permute-start | bytes 1474568 | tf_op jit(solution)/shard_map/ppermute | solution.py:227
  39.1 12.6 %all-to-all-start.1 = ((bf16[8,4,5120]{2,1,0:T(4,128)(2,1)}), bf16[8,4,5120]{2,1,0:T(4,128)(2,1)}, u32[]{:S(2)}, u32[]{:S(2)}) async-start(bf16[8,4,5120]{2,1,0:T(4,128)(2,1)} %attention.1), calls=%async_computation.1 | async-start | bytes 655360 | tf_op jit(solution)/shard_map/all_to_all | solution.py:255
  44.0 12.3 %collective-permute-start.4 = (bf16[8,40,768]{2,1,0:T(8,128)(2,1)S(1)}, bf16[8,40,768]{2,1,0:T(8,128)(2,1)}, u32[]{:S(2)}, u32[]{:S(2)}) collective-permute-start(bf16[8,40,768]{2,1,0:T(8,128)(2,1)S(1)} %collective-permute-done.3.refs_2_), channel_id=1, source_target_pairs={{0,8},{8,0},{1,9},{9,1},{2,10},{10,2},{3,11},{11,3},{4,12},{12,4},... | collective-permute-start | bytes 1474568 | tf_op jit(solution)/shard_map/ppermute | solution.py:220
  45.1 17.6 %collective-permute-start.11 = (bf16[8,40,768]{2,1,0:T(8,128)(2,1)S(1)}, bf16[8,40,768]{2,1,0:T(8,128)(2,1)}, u32[]{:S(2)}, u32[]{:S(2)}) collective-permute-start(bf16[8,40,768]{2,1,0:T(8,128)(2,1)S(1)} %collective-permute-done.7.refs_4_), channel_id=1, source_target_pairs={{0,64},{64,0},{1,65},{65,1},{2,66},{66,2},{3,67},{67,3},{4,68},{68... | collective-permute-start | bytes 1474568 | tf_op jit(solution)/shard_map/ppermute | solution.py:220
  48.5 7.9 %collective-permute-start.2 = (bf16[8,40,768]{2,1,0:T(8,128)(2,1)S(1)}, bf16[8,40,768]{2,1,0:T(8,128)(2,1)}, u32[]{:S(2)}, u32[]{:S(2)}) collective-permute-start(bf16[8,40,768]{2,1,0:T(8,128)(2,1)S(1)} %collective-permute-done.1.refs_0_), channel_id=1, source_target_pairs={{0,8},{8,0},{1,9},{9,1},{2,10},{10,2},{3,11},{11,3},{4,12},{12,4},... | collective-permute-start | bytes 1474568 | tf_op jit(solution)/shard_map/ppermute | solution.py:220
  51.7 4.7 %collective-permute-start.10 = (bf16[8,40,768]{2,1,0:T(8,128)(2,1)S(1)}, bf16[8,40,768]{2,1,0:T(8,128)(2,1)S(1)}, u32[]{:S(2)}, u32[]{:S(2)}) collective-permute-start(bf16[8,40,768]{2,1,0:T(8,128)(2,1)S(1)} %collective-permute-done.9.refs_4_), channel_id=1, source_target_pairs={{0,8},{8,0},{1,9},{9,1},{2,10},{10,2},{3,11},{11,3},{4,12},{12,4},... | collective-permute-start | bytes 1474568 | tf_op jit(solution)/shard_map/ppermute | solution.py:220
  52.7 10.1 %collective-permute-start.12 = (bf16[8,40,768]{2,1,0:T(8,128)(2,1)S(1)}, bf16[8,40,768]{2,1,0:T(8,128)(2,1)S(1)}, u32[]{:S(2)}, u32[]{:S(2)}) collective-permute-start(bf16[8,40,768]{2,1,0:T(8,128)(2,1)S(1)} %collective-permute-done.9.refs_4_), channel_id=1, source_target_pairs={{0,16},{8,56},{16,32},{24,8},{32,48},{40,24},{48,0},{56,40},{1,17}... | collective-permute-start | bytes 1474568 | tf_op jit(solution)/shard_map/ppermute | solution.py:227
  62.8 3.4 %collective-permute-start.13 = (bf16[8,40,768]{2,1,0:T(8,128)(2,1)}, bf16[8,40,768]{2,1,0:T(8,128)(2,1)S(1)}, u32[]{:S(2)}, u32[]{:S(2)}) collective-permute-start(bf16[8,40,768]{2,1,0:T(8,128)(2,1)} %collective-permute-done.11.refs_0_), channel_id=1, source_target_pairs={{0,8},{8,0},{1,9},{9,1},{2,10},{10,2},{3,11},{11,3},{4,12},{12,4},... | collective-permute-start | bytes 1474568 | tf_op jit(solution)/shard_map/ppermute | solution.py:220
  63.8 2.4 %collective-permute-start.14 = (bf16[8,40,768]{2,1,0:T(8,128)(2,1)S(1)}, bf16[8,40,768]{2,1,0:T(8,128)(2,1)S(1)}, u32[]{:S(2)}, u32[]{:S(2)}) collective-permute-start(bf16[8,40,768]{2,1,0:T(8,128)(2,1)S(1)} %collective-permute-done.12.refs_1_), channel_id=1, source_target_pairs={{0,8},{8,0},{1,9},{9,1},{2,10},{10,2},{3,11},{11,3},{4,12},{12,4},... | collective-permute-start | bytes 1474568 | tf_op jit(solution)/shard_map/ppermute | solution.py:220

commit v3 on v2

--- a/solution.py
+++ b/solution.py
@@ -251,38 +251,34 @@
     core_own = swap(own, "core")
     near = ring(own)
     near_pair = ring(core_own)
-    near, partial = lax.optimization_barrier((near, partial))
-    terms = lax.all_to_all(partial, TP, split_axis=0, concat_axis=0, tiled=True)
-    far = ring(near)
-    core_near = swap(near, "core")
-    other_near_pair = swap(near_pair, "z_hi")
-    core_near_pair = swap(near_pair, "core")
-    core_far = swap(far, "core")
-    other_near = ring(other)
-    core_other = swap(other, "core")
     out = place(
         [
             (own, 0, tp, slot(0, 0, 0), 0),
             (core_own, 0, tp, slot(0, 0, 1), 0),
             (near, 0, tp, slot(0, back, 0), 0),
-            (core_near, 0, tp, slot(0, -back, 1), 0),
-            (near_pair, 0, tp, slot(0, back, 1), 0),
-            (core_near_pair, 0, tp, slot(0, -back, 0), 0),
         ],
         shape,
     )
-    out, terms, other_near = lax.optimization_barrier((out, terms, other_near))
-    other_far = ring(other_near)
+    far = ring(near)
+    core_near = swap(near, "core")
+    core_near_pair = swap(near_pair, "core")
+    core_far = swap(far, "core")
+    other_far = swap(far, "z_hi")
+    other, near_pair, out = lax.optimization_barrier((other, near_pair, out))
+    other_near = ring(other)
+    core_other = swap(other, "core")
+    core_other, partial = lax.optimization_barrier((core_other, partial))
+    terms = lax.all_to_all(partial, TP, split_axis=0, concat_axis=0, tiled=True)
+    other_near_pair = ring(core_other)
     core_other_near = swap(other_near, "core")
-    attended = terms[0].astype(F32)
-    for peer in range(1, tp):
-        attended = attended + terms[peer].astype(F32)
-    attended = attended.astype(BF16)
     out = place(
         [
+            (near_pair, 0, tp, slot(0, back, 1), 0),
+            (core_near, 0, tp, slot(0, -back, 1), 0),
+            (core_near_pair, 0, tp, slot(0, -back, 0), 0),
+            (other, 0, tp, slot(1, 0, 0), 0),
             (far, 0, tp, slot(0, 2, 0), 0),
             (core_far, 0, tp, slot(0, 2, 1), 0),
-            (other, 0, tp, slot(1, 0, 0), 0),
             (core_other, 0, tp, slot(1, 0, 1), 0),
             (other_near, 0, tp, slot(1, back, 0), 0),
             (core_other_near, 0, tp, slot(1, -back, 1), 0),
@@ -290,9 +286,13 @@
         shape,
         out,
     )
-    out, attended, other_near_pair, other_far = lax.optimization_barrier((out, attended, other_near_pair, other_far))
+    out, other_near_pair, other_far = lax.optimization_barrier((out, other_near_pair, other_far))
     core_other_near_pair = swap(other_near_pair, "core")
     core_other_far = swap(other_far, "core")
+    attended = terms[0].astype(F32)
+    for peer in range(1, tp):
+        attended = attended + terms[peer].astype(F32)
+    attended = attended.astype(BF16)
     out = place(
         [
             (other_near_pair, 0, tp, slot(1, back, 1), 0),

time: 69 us -> 64.8 us (0.939)
  waiting for transfers between devices: 11.7 us -> 7.78 us
  local copies, waits for them, and re-layouts: 2.01 us -> 3.74 us
  Pallas kernels: 16.5 us -> 15.5 us
  starting transfers between devices: 34.4 us -> 33.4 us
    ppermute x10, waiting for transfers between devices: 8.82 us -> 3.22 us  [swap(): return lax.ppermute(array, axis, [(0, 1), (1, 0)])]
    all_to_all x1, waiting for transfers between devices: 0.01 us -> 2.14 us  [body(): terms = lax.all_to_all(partial, TP, split_axis=0, concat_axis=0, tiled=True)]
    ppermute x10, starting transfers between devices: 14.9 us -> 12.9 us  [swap(): return lax.ppermute(array, axis, [(0, 1), (1, 0)])]
    unnamed x0 -> x4, local copies, waits for them, and re-layouts: none -> 1.81 us
    pallas_call x3, Pallas kernels: 8.01 us -> 7 us  [place(): pl.pallas_call(kernel, out_shape=jax.ShapeDtypeStruct(shape, BF16), in_sp...]
  transfers between devices with their start and end apart: 17 -> 17, of which waited for: 5 -> 4; matrix products, arithmetic and copies ran while one was open for 4% -> 4% of each run, Pallas kernels for 21% -> 21%
where the time goes in v3:
time: 64.8 us; the launch traced here: 64.3 us
  starting transfers between devices  33.4 us (52%)
  Pallas kernels  15.5 us (24%)
  waiting for transfers between devices  7.78 us (12%)
  local copies, waits for them, and re-layouts  3.74 us (6%)
  other arithmetic  2.56 us (4%)
  between operations  1.38 us (2%)
    ppermute x10, starting transfers between devices, swap(): return lax.ppermute(array, axis, [(0, 1), (1, 0)])  12.9 us
    ppermute x5, starting transfers between devices, ring(): return lax.ppermute(array, ('x', 'core'), pairs)  9 us
    pallas_call x1, Pallas kernels, attention(): pl.pallas_call(attention_kernel, out_shape=jax.ShapeDtypeStruct((tp, STEP...  8.49 us
    pallas_call x3, Pallas kernels, place(): pl.pallas_call(kernel, out_shape=jax.ShapeDtypeStruct(shape, BF16), in_sp...  7 us
    all_to_all x1, starting transfers between devices, body(): own = lax.all_to_all(blocks, TP, split_axis=0, concat_axis=0, tiled=True)  6.37 us
    all_to_all x1, starting transfers between devices, body(): terms = lax.all_to_all(partial, TP, split_axis=0, concat_axis=0, tiled=True)  5.06 us
    ppermute x10, waiting for transfers between devices, swap(): return lax.ppermute(array, axis, [(0, 1), (1, 0)])  3.22 us
    ppermute x5, waiting for transfers between devices, ring(): return lax.ppermute(array, ('x', 'core'), pairs)  2.42 us
  transfers between devices with their start and end apart: 17, of which 4 were waited for; matrix products, arithmetic and copies ran while one was open for 4% of the time, Pallas kernels for 21%

profile of v3, /device:TPU:1, one launch (start us, length us, event | category | flops | bytes accessed | tf_op | source)
XLA Modules:
  0.0 64.3 jit_solution(13973133784624689175)
XLA Ops:
  0.6 1.8 %copy.17 = bf16[5,8,8,768]{3,2,0,1:T(8,128)(2,1)} copy(bf16[5,8,8,768]{3,2,1,0:T(8,128)(2,1)} %bitcast.32) | data formatting | bytes 983040 | tf_op jit(solution)/shard_map/reshape | solution.py:242
  2.5 6.4 %all-to-all-start = ((bf16[8,40,768]{2,1,0:T(8,128)(2,1)}), bf16[8,40,768]{2,1,0:T(8,128)(2,1)S(1)}, u32[]{:S(2)}, u32[]{:S(2)}) async-start(bf16[8,40,768]{2,1,0:T(8,128)(2,1)} %bitcast.27), calls=%async_computation | async-start | bytes 983040 | tf_op jit(solution)/shard_map/all_to_all | solution.py:243
  9.6 0.7 %pad_maximum_fusion = (f32[4,128]{1,0:T(4,128)}, f32[4,128]{1,0:T(4,128)}) fusion(f32[4,64]{1,0:T(4,128)S(1)} %get-tuple-element.24, f32[4,64]{1,0:T(4,128)S(1)} %get-tuple-element.23, f32[4,64]{1,0:T(4,128)S(1)} %get-tuple-element.22), kind=kLoop, calls=%fused_computation.4 | loop fusion | flops 1024 | bytes 7168 | tf_op jit(solution)/shard_map/concatenate | solution.py:25
  10.3 8.5 %attention.1 = bf16[8,4,5120]{2,1,0:T(4,128)(2,1)} custom-call(s32[1]{0:T(128)} %copy.20.length_ref, f32[4,128]{1,0:T(4,128)} %get-tuple-element.25.cos_ref, f32[4,128]{1,0:T(4,128)} %get-tuple-element.26.sin_ref, bf16[4,5120]{1,0:T(4,128)(2,1)} %bitcast.33, bf16[5120]{0:T(1024)(128)(2,1)} %in_gain_hbm.1, bf16[128]{0:T(256)(128)(2,1)} %q_gain_hbm.1, ...), custom_call_target="tpu_custom_call" | custom-call | flops 120000000 | bytes 17400000 | tf_op jit(solution)/shard_map/attention/pallas_call | solution.py:152
  18.8 1.0 %collective-permute-start.1 = (bf16[8,40,768]{2,1,0:T(8,128)(2,1)S(1)}, bf16[8,40,768]{2,1,0:T(8,128)(2,1)S(1)}, u32[]{:S(2)}, u32[]{:S(2)}) collective-permute-start(bf16[8,40,768]{2,1,0:T(8,128)(2,1)S(1)} %all-to-all-done.refs_0_), channel_id=1, source_target_pairs={{0,8},{8,0},{1,9},{9,1},{2,10},{10,2},{3,11},{11,3},{4,12},{12,4},... | collective-permute-start | bytes 1474568 | tf_op jit(solution)/shard_map/ppermute | solution.py:220
  19.8 2.5 %collective-permute-start.3 = (bf16[8,40,768]{2,1,0:T(8,128)(2,1)S(1)}, bf16[8,40,768]{2,1,0:T(8,128)(2,1)S(1)}, u32[]{:S(2)}, u32[]{:S(2)}) collective-permute-start(bf16[8,40,768]{2,1,0:T(8,128)(2,1)S(1)} %all-to-all-done.refs_0_), channel_id=1, source_target_pairs={{0,16},{8,56},{16,32},{24,8},{32,48},{40,24},{48,0},{56,40},{1,17}... | collective-permute-start | bytes 1474568 | tf_op jit(solution)/shard_map/ppermute | solution.py:227
  22.3 3.3 %collective-permute-start = (bf16[8,40,768]{2,1,0:T(8,128)(2,1)S(1)}, bf16[8,40,768]{2,1,0:T(8,128)(2,1)S(1)}, u32[]{:S(2)}, u32[]{:S(2)}) collective-permute-start(bf16[8,40,768]{2,1,0:T(8,128)(2,1)S(1)} %all-to-all-done.refs_0_), channel_id=1, source_target_pairs={{0,64},{64,0},{1,65},{65,1},{2,66},{66,2},{3,67},{67,3},{4,68},{68... | collective-permute-start | bytes 1474568 | tf_op jit(solution)/shard_map/ppermute | solution.py:220
  26.2 1.8 %collective-permute-done.3.refs_2_ = bf16[8,40,768]{2,1,0:T(8,128)(2,1)S(1)} collective-permute-done((bf16[8,40,768]{2,1,0:T(8,128)(2,1)S(1)}, bf16[8,40,768]{2,1,0:T(8,128)(2,1)S(1)}, u32[]{:S(2)}, u32[]{:S(2)}) %collective-permute-start.3) | collective-permute-done | bytes 491552 | tf_op jit(solution)/shard_map/ppermute | solution.py:227
  28.1 3.4 %collective-permute-start.7 = (bf16[8,40,768]{2,1,0:T(8,128)(2,1)S(1)}, bf16[8,40,768]{2,1,0:T(8,128)(2,1)S(1)}, u32[]{:S(2)}, u32[]{:S(2)}) collective-permute-start(bf16[8,40,768]{2,1,0:T(8,128)(2,1)S(1)} %collective-permute-done.3.refs_2_), channel_id=1, source_target_pairs={{0,16},{8,56},{16,32},{24,8},{32,48},{40,24},{48,0},{56,40},{1,17}... | collective-permute-start | bytes 1474568 | tf_op jit(solution)/shard_map/ppermute | solution.py:227
  31.5 1.7 %place.3.refs_9_ = bf16[16,8,40,768]{3,2,1,0:T(8,128)(2,1)} custom-call(s32[3]{0:T(128)S(1)} %pad_add_fusion.slots_ref, bf16[8,40,768]{2,1,0:T(8,128)(2,1)S(1)} %all-to-all-done.refs_0_, bf16[8,40,768]{2,1,0:T(8,128)(2,1)S(1)} %collective-permute-done.1.refs_1_, bf16[8,40,768]{2,1,0:T(8,128)(2,1)S(1)} %collective-permute-done.3.refs_2_), custom_call_target="tpu_custom_call" | custom-call | bytes 2949120 | tf_op jit(solution)/shard_map/place/pallas_call | solution.py:204
  33.2 3.2 %collective-permute-done.refs_3_ = bf16[8,40,768]{2,1,0:T(8,128)(2,1)S(1)} collective-permute-done((bf16[8,40,768]{2,1,0:T(8,128)(2,1)S(1)}, bf16[8,40,768]{2,1,0:T(8,128)(2,1)S(1)}, u32[]{:S(2)}, u32[]{:S(2)}) %collective-permute-start) | collective-permute-done | bytes 491552 | tf_op jit(solution)/shard_map/ppermute | solution.py:220
  36.4 2.0 %collective-permute-start.9 = (bf16[8,40,768]{2,1,0:T(8,128)(2,1)S(1)}, bf16[8,40,768]{2,1,0:T(8,128)(2,1)S(1)}, u32[]{:S(2)}, u32[]{:S(2)}) collective-permute-start(bf16[8,40,768]{2,1,0:T(8,128)(2,1)S(1)} %collective-permute-done.refs_3_), channel_id=1, source_target_pairs={{0,16},{8,56},{16,32},{24,8},{32,48},{40,24},{48,0},{56,40},{1,17}... | collective-permute-start | bytes 1474568 | tf_op jit(solution)/shard_map/ppermute | solution.py:227
  38.9 1.6 %collective-permute-start.8 = (bf16[8,40,768]{2,1,0:T(8,128)(2,1)S(1)}, bf16[8,40,768]{2,1,0:T(8,128)(2,1)}, u32[]{:S(2)}, u32[]{:S(2)}) collective-permute-start(bf16[8,40,768]{2,1,0:T(8,128)(2,1)S(1)} %collective-permute-done.7.refs_4_), channel_id=1, source_target_pairs={{0,8},{8,0},{1,9},{9,1},{2,10},{10,2},{3,11},{11,3},{4,12},{12,4},... | collective-permute-start | bytes 1474568 | tf_op jit(solution)/shard_map/ppermute | solution.py:220
  40.5 3.3 %collective-permute-start.12 = (bf16[8,40,768]{2,1,0:T(8,128)(2,1)S(1)}, bf16[8,40,768]{2,1,0:T(8,128)(2,1)S(1)}, u32[]{:S(2)}, u32[]{:S(2)}) collective-permute-start(bf16[8,40,768]{2,1,0:T(8,128)(2,1)S(1)} %collective-permute-done.7.refs_4_), channel_id=1, source_target_pairs={{0,64},{64,0},{1,65},{65,1},{2,66},{66,2},{3,67},{67,3},{4,68},{68... | collective-permute-start | bytes 1474568 | tf_op jit(solution)/shard_map/ppermute | solution.py:220
  43.8 0.6 collective-permute-done.9.refs_7_
  44.4 2.6 %collective-permute-start.10 = (bf16[8,40,768]{2,1,0:T(8,128)(2,1)S(1)}, bf16[8,40,768]{2,1,0:T(8,128)(2,1)}, u32[]{:S(2)}, u32[]{:S(2)}) collective-permute-start(bf16[8,40,768]{2,1,0:T(8,128)(2,1)S(1)} %collective-permute-done.9.refs_7_), channel_id=1, source_target_pairs={{0,8},{8,0},{1,9},{9,1},{2,10},{10,2},{3,11},{11,3},{4,12},{12,4},... | collective-permute-start | bytes 1474568 | tf_op jit(solution)/shard_map/ppermute | solution.py:220
  46.9 0.8 %copy-done = bf16[8,40,768]{2,1,0:T(8,128)(2,1)} copy-done((bf16[8,40,768]{2,1,0:T(8,128)(2,1)}, bf16[8,40,768]{2,1,0:T(8,128)(2,1)S(1)}, u32[]{:S(2)}) %copy-start) | copy-done | bytes 491544
  47.7 0.6 collective-permute-start.11
  48.3 5.1 %all-to-all-start.1 = ((bf16[8,4,5120]{2,1,0:T(4,128)(2,1)}), bf16[8,4,5120]{2,1,0:T(4,128)(2,1)}, u32[]{:S(2)}, u32[]{:S(2)}) async-start(bf16[8,4,5120]{2,1,0:T(4,128)(2,1)} %attention.1), calls=%async_computation.1 | async-start | bytes 655360 | tf_op jit(solution)/shard_map/all_to_all | solution.py:271
  53.6 1.0 %copy-done.1 = bf16[8,40,768]{2,1,0:T(8,128)(2,1)S(1)} copy-done((bf16[8,40,768]{2,1,0:T(8,128)(2,1)S(1)}, bf16[8,40,768]{2,1,0:T(8,128)(2,1)}, u32[]{:S(2)}) %copy-start.1) | copy-done | bytes 491544
  54.6 3.5 %place.4.refs_4_ = bf16[16,8,40,768]{3,2,1,0:T(8,128)(2,1)} custom-call(s32[9]{0:T(128)S(1)} %stack.75.slots_ref, bf16[8,40,768]{2,1,0:T(8,128)(2,1)S(1)} %collective-permute-done.2.refs_0_, bf16[8,40,768]{2,1,0:T(8,128)(2,1)S(1)} %copy-done.1, bf16[8,40,768]{2,1,0:T(8,128)(2,1)} %collective-permute-done.6.refs_2_, ...), custom_call_target="tpu_custom_call", output_to_operand_aliasing={{}: (10, {})} | custom-call | bytes 8847360 | tf_op jit(solution)/shard_map/place/pallas_call | solution.py:204
  58.7 2.1 %all-to-all-done.1 = bf16[8,4,5120]{2,1,0:T(4,128)(2,1)} async-done(((bf16[8,4,5120]{2,1,0:T(4,128)(2,1)}), bf16[8,4,5120]{2,1,0:T(4,128)(2,1)}, u32[]{:S(2)}, u32[]{:S(2)}) %all-to-all-start.1) | async-done | bytes 327712 | tf_op jit(solution)/shard_map/all_to_all | solution.py:271
  60.8 1.6 %add_convert_fusion = bf16[1,4,5120]{2,1,0:T(4,128)(2,1)} fusion(bf16[8,4,5120]{2,1,0:T(4,128)(2,1)} %all-to-all-done.1), kind=kLoop, calls=%fused_computation.1 | loop fusion | flops 327680 | bytes 368640 | tf_op jit(solution)/shard_map/convert_element_type | solution.py:295
  62.5 1.8 %place.5 = bf16[16,8,40,768]{3,2,1,0:T(8,128)(2,1)} custom-call(s32[4]{0:T(128)S(1)} %pad_add_fusion.1.slots_ref, bf16[8,40,768]{2,1,0:T(8,128)(2,1)S(1)} %collective-permute-done.11.refs_0_, bf16[8,40,768]{2,1,0:T(8,128)(2,1)S(1)} %collective-permute-done.12.refs_1_, ...), custom_call_target="tpu_custom_call", output_to_operand_aliasing={{}: (5, {})} | custom-call | bytes 3932160 | tf_op jit(solution)/shard_map/place/pallas_call | solution.py:204
  (27 shorter events, 2.1 us)
Async XLA Ops:
  2.5 16.3 %all-to-all-start = ((bf16[8,40,768]{2,1,0:T(8,128)(2,1)}), bf16[8,40,768]{2,1,0:T(8,128)(2,1)S(1)}, u32[]{:S(2)}, u32[]{:S(2)}) async-start(bf16[8,40,768]{2,1,0:T(8,128)(2,1)} %bitcast.27), calls=%async_computation | async-start | bytes 983040 | tf_op jit(solution)/shard_map/all_to_all | solution.py:243
  18.8 6.8 %collective-permute-start.1 = (bf16[8,40,768]{2,1,0:T(8,128)(2,1)S(1)}, bf16[8,40,768]{2,1,0:T(8,128)(2,1)S(1)}, u32[]{:S(2)}, u32[]{:S(2)}) collective-permute-start(bf16[8,40,768]{2,1,0:T(8,128)(2,1)S(1)} %all-to-all-done.refs_0_), channel_id=1, source_target_pairs={{0,8},{8,0},{1,9},{9,1},{2,10},{10,2},{3,11},{11,3},{4,12},{12,4},... | collective-permute-start | bytes 1474568 | tf_op jit(solution)/shard_map/ppermute | solution.py:220
  19.8 8.3 %collective-permute-start.3 = (bf16[8,40,768]{2,1,0:T(8,128)(2,1)S(1)}, bf16[8,40,768]{2,1,0:T(8,128)(2,1)S(1)}, u32[]{:S(2)}, u32[]{:S(2)}) collective-permute-start(bf16[8,40,768]{2,1,0:T(8,128)(2,1)S(1)} %all-to-all-done.refs_0_), channel_id=1, source_target_pairs={{0,16},{8,56},{16,32},{24,8},{32,48},{40,24},{48,0},{56,40},{1,17}... | collective-permute-start | bytes 1474568 | tf_op jit(solution)/shard_map/ppermute | solution.py:227
  22.3 14.1 %collective-permute-start = (bf16[8,40,768]{2,1,0:T(8,128)(2,1)S(1)}, bf16[8,40,768]{2,1,0:T(8,128)(2,1)S(1)}, u32[]{:S(2)}, u32[]{:S(2)}) collective-permute-start(bf16[8,40,768]{2,1,0:T(8,128)(2,1)S(1)} %all-to-all-done.refs_0_), channel_id=1, source_target_pairs={{0,64},{64,0},{1,65},{65,1},{2,66},{66,2},{3,67},{67,3},{4,68},{68... | collective-permute-start | bytes 1474568 | tf_op jit(solution)/shard_map/ppermute | solution.py:220
  25.6 10.8 %collective-permute-start.2 = (bf16[8,40,768]{2,1,0:T(8,128)(2,1)S(1)}, bf16[8,40,768]{2,1,0:T(8,128)(2,1)S(1)}, u32[]{:S(2)}, u32[]{:S(2)}) collective-permute-start(bf16[8,40,768]{2,1,0:T(8,128)(2,1)S(1)} %collective-permute-done.1.refs_1_), channel_id=1, source_target_pairs={{0,16},{8,56},{16,32},{24,8},{32,48},{40,24},{48,0},{56,40},{1,17}... | collective-permute-start | bytes 1474568 | tf_op jit(solution)/shard_map/ppermute | solution.py:227
  28.1 10.8 %collective-permute-start.7 = (bf16[8,40,768]{2,1,0:T(8,128)(2,1)S(1)}, bf16[8,40,768]{2,1,0:T(8,128)(2,1)S(1)}, u32[]{:S(2)}, u32[]{:S(2)}) collective-permute-start(bf16[8,40,768]{2,1,0:T(8,128)(2,1)S(1)} %collective-permute-done.3.refs_2_), channel_id=1, source_target_pairs={{0,16},{8,56},{16,32},{24,8},{32,48},{40,24},{48,0},{56,40},{1,17}... | collective-permute-start | bytes 1474568 | tf_op jit(solution)/shard_map/ppermute | solution.py:227
  36.4 4.1 %collective-permute-start.4 = (bf16[8,40,768]{2,1,0:T(8,128)(2,1)S(1)}, bf16[8,40,768]{2,1,0:T(8,128)(2,1)S(1)}, u32[]{:S(2)}, u32[]{:S(2)}) collective-permute-start(bf16[8,40,768]{2,1,0:T(8,128)(2,1)S(1)} %collective-permute-done.refs_3_), channel_id=1, source_target_pairs={{0,8},{8,0},{1,9},{9,1},{2,10},{10,2},{3,11},{11,3},{4,12},{12,4},... | collective-permute-start | bytes 1474568 | tf_op jit(solution)/shard_map/ppermute | solution.py:220
  36.4 8.0 %collective-permute-start.9 = (bf16[8,40,768]{2,1,0:T(8,128)(2,1)S(1)}, bf16[8,40,768]{2,1,0:T(8,128)(2,1)S(1)}, u32[]{:S(2)}, u32[]{:S(2)}) collective-permute-start(bf16[8,40,768]{2,1,0:T(8,128)(2,1)S(1)} %collective-permute-done.refs_3_), channel_id=1, source_target_pairs={{0,16},{8,56},{16,32},{24,8},{32,48},{40,24},{48,0},{56,40},{1,17}... | collective-permute-start | bytes 1474568 | tf_op jit(solution)/shard_map/ppermute | solution.py:227
  38.3 8.6 %collective-permute-start.5 = (bf16[8,40,768]{2,1,0:T(8,128)(2,1)S(1)}, bf16[8,40,768]{2,1,0:T(8,128)(2,1)S(1)}, u32[]{:S(2)}, u32[]{:S(2)}) collective-permute-start(bf16[8,40,768]{2,1,0:T(8,128)(2,1)S(1)} %collective-permute-done.3.refs_2_), channel_id=1, source_target_pairs={{0,8},{8,0},{1,9},{9,1},{2,10},{10,2},{3,11},{11,3},{4,12},{12,4},... | collective-permute-start | bytes 1474568 | tf_op jit(solution)/shard_map/ppermute | solution.py:220
  38.4 15.2 %collective-permute-start.6 = (bf16[8,40,768]{2,1,0:T(8,128)(2,1)S(1)}, bf16[8,40,768]{2,1,0:T(8,128)(2,1)}, u32[]{:S(2)}, u32[]{:S(2)}) collective-permute-start(bf16[8,40,768]{2,1,0:T(8,128)(2,1)S(1)} %collective-permute-done.2.refs_0_), channel_id=1, source_target_pairs={{0,8},{8,0},{1,9},{9,1},{2,10},{10,2},{3,11},{11,3},{4,12},{12,4},... | collective-permute-start | bytes 1474568 | tf_op jit(solution)/shard_map/ppermute | solution.py:220
  38.9 14.7 %collective-permute-start.8 = (bf16[8,40,768]{2,1,0:T(8,128)(2,1)S(1)}, bf16[8,40,768]{2,1,0:T(8,128)(2,1)}, u32[]{:S(2)}, u32[]{:S(2)}) collective-permute-start(bf16[8,40,768]{2,1,0:T(8,128)(2,1)S(1)} %collective-permute-done.7.refs_4_), channel_id=1, source_target_pairs={{0,8},{8,0},{1,9},{9,1},{2,10},{10,2},{3,11},{11,3},{4,12},{12,4},... | collective-permute-start | bytes 1474568 | tf_op jit(solution)/shard_map/ppermute | solution.py:220
  40.5 17.6 %collective-permute-start.12 = (bf16[8,40,768]{2,1,0:T(8,128)(2,1)S(1)}, bf16[8,40,768]{2,1,0:T(8,128)(2,1)S(1)}, u32[]{:S(2)}, u32[]{:S(2)}) collective-permute-start(bf16[8,40,768]{2,1,0:T(8,128)(2,1)S(1)} %collective-permute-done.7.refs_4_), channel_id=1, source_target_pairs={{0,64},{64,0},{1,65},{65,1},{2,66},{66,2},{3,67},{67,3},{4,68},{68... | collective-permute-start | bytes 1474568 | tf_op jit(solution)/shard_map/ppermute | solution.py:220
  44.4 9.2 %collective-permute-start.10 = (bf16[8,40,768]{2,1,0:T(8,128)(2,1)S(1)}, bf16[8,40,768]{2,1,0:T(8,128)(2,1)}, u32[]{:S(2)}, u32[]{:S(2)}) collective-permute-start(bf16[8,40,768]{2,1,0:T(8,128)(2,1)S(1)} %collective-permute-done.9.refs_7_), channel_id=1, source_target_pairs={{0,8},{8,0},{1,9},{9,1},{2,10},{10,2},{3,11},{11,3},{4,12},{12,4},... | collective-permute-start | bytes 1474568 | tf_op jit(solution)/shard_map/ppermute | solution.py:220
  46.9 0.8 %copy-start = (bf16[8,40,768]{2,1,0:T(8,128)(2,1)}, bf16[8,40,768]{2,1,0:T(8,128)(2,1)S(1)}, u32[]{:S(2)}) copy-start(bf16[8,40,768]{2,1,0:T(8,128)(2,1)S(1)} %collective-permute-done.5.refs_1_) | copy-start | bytes 1474564
  47.7 10.4 %collective-permute-start.11 = (bf16[8,40,768]{2,1,0:T(8,128)(2,1)S(1)}, bf16[8,40,768]{2,1,0:T(8,128)(2,1)S(1)}, u32[]{:S(2)}, u32[]{:S(2)}) collective-permute-start(bf16[8,40,768]{2,1,0:T(8,128)(2,1)S(1)} %collective-permute-done.4.refs_6_), channel_id=1, source_target_pairs={{0,16},{8,56},{16,32},{24,8},{32,48},{40,24},{48,0},{56,40},{1,17}... | collective-permute-start | bytes 1474568 | tf_op jit(solution)/shard_map/ppermute | solution.py:227
  48.3 12.5 %all-to-all-start.1 = ((bf16[8,4,5120]{2,1,0:T(4,128)(2,1)}), bf16[8,4,5120]{2,1,0:T(4,128)(2,1)}, u32[]{:S(2)}, u32[]{:S(2)}) async-start(bf16[8,4,5120]{2,1,0:T(4,128)(2,1)} %attention.1), calls=%async_computation.1 | async-start | bytes 655360 | tf_op jit(solution)/shard_map/all_to_all | solution.py:271
  53.6 1.0 %copy-start.1 = (bf16[8,40,768]{2,1,0:T(8,128)(2,1)S(1)}, bf16[8,40,768]{2,1,0:T(8,128)(2,1)}, u32[]{:S(2)}) copy-start(bf16[8,40,768]{2,1,0:T(8,128)(2,1)} %copy-done) | copy-start | bytes 1474564
  58.1 4.4 %collective-permute-start.13 = (bf16[8,40,768]{2,1,0:T(8,128)(2,1)S(1)}, bf16[8,40,768]{2,1,0:T(8,128)(2,1)S(1)}, u32[]{:S(2)}, u32[]{:S(2)}) collective-permute-start(bf16[8,40,768]{2,1,0:T(8,128)(2,1)S(1)} %collective-permute-done.11.refs_0_), channel_id=1, source_target_pairs={{0,8},{8,0},{1,9},{9,1},{2,10},{10,2},{3,11},{11,3},{4,12},{12,4},... | collective-permute-start | bytes 1474568 | tf_op jit(solution)/shard_map/ppermute | solution.py:220
  58.5 4.0 %collective-permute-start.14 = (bf16[8,40,768]{2,1,0:T(8,128)(2,1)S(1)}, bf16[8,40,768]{2,1,0:T(8,128)(2,1)S(1)}, u32[]{:S(2)}, u32[]{:S(2)}) collective-permute-start(bf16[8,40,768]{2,1,0:T(8,128)(2,1)S(1)} %collective-permute-done.12.refs_1_), channel_id=1, source_target_pairs={{0,8},{8,0},{1,9},{9,1},{2,10},{10,2},{3,11},{11,3},{4,12},{12,4},... | collective-permute-start | bytes 1474568 | tf_op jit(solution)/shard_map/ppermute | solution.py:220

commit v4 on v3

--- a/solution.py
+++ b/solution.py
@@ -12,7 +12,7 @@
 HEAD = 128
 ROWS = STEPS * GROUP
 REP = ("z_hi", "x", "core")
-TP = "tp"
+TP = ("y", "z_lo")
 
 
 def rope_tables(cache_lengths):
@@ -139,11 +139,10 @@
             preferred_element_type=F32,
         )
         partial = term if partial is None else partial + term
-    for peer in range(partial_ref.shape[0]):
-        partial_ref[peer] = partial.astype(BF16)
-
-
-def attention(hidden, in_gain, old_qkv, old_out, q_gain, k_gain, cache_keys, stored_values, cache_lengths, tp):
+    partial_ref[...] = partial.astype(BF16)
+
+
+def attention(hidden, in_gain, old_qkv, old_out, q_gain, k_gain, cache_keys, stored_values, cache_lengths):
     width = hidden.shape[-1]
     slots = cache_keys.shape[1]
     cosine, sine = rope_tables(cache_lengths)
@@ -151,7 +150,7 @@
     hbm = pl.BlockSpec(memory_space=pltpu.HBM)
     return pl.pallas_call(
         attention_kernel,
-        out_shape=jax.ShapeDtypeStruct((tp, STEPS, width), BF16),
+        out_shape=jax.ShapeDtypeStruct((STEPS, width), BF16),
         in_specs=[pl.BlockSpec(memory_space=pltpu.SMEM)] + [vmem] * 2 + [hbm] * 8,
         out_specs=vmem,
         scratch_shapes=[
@@ -242,7 +241,7 @@
     blocks = new_qkv.reshape(rows, tp, columns // tp).transpose(1, 0, 2)
     own = lax.all_to_all(blocks, TP, split_axis=0, concat_axis=0, tiled=True)
     partial = attention(
-        hidden, in_gain, old_qkv, old_out, q_gain, k_gain, cache_keys, stored_values, cache_lengths, tp
+        hidden, in_gain, old_qkv, old_out, q_gain, k_gain, cache_keys, stored_values, cache_lengths
     )
     own, partial = lax.optimization_barrier((own, partial))
     shape = (rep, tp, rows, columns // tp)
@@ -250,6 +249,10 @@
     other = swap(own, "z_hi")
     core_own = swap(own, "core")
     near = ring(own)
+    near, partial = lax.optimization_barrier((near, partial))
+    pair = swap(partial, "z_lo")
+    partial = (partial.astype(F32) + pair.astype(F32)).astype(BF16)
+    partial = jnp.broadcast_to(partial[None], (4,) + partial.shape)
     near_pair = ring(core_own)
     out = place(
         [
@@ -268,36 +271,36 @@
     other_near = ring(other)
     core_other = swap(other, "core")
     core_other, partial = lax.optimization_barrier((core_other, partial))
-    terms = lax.all_to_all(partial, TP, split_axis=0, concat_axis=0, tiled=True)
+    terms = lax.all_to_all(partial, "y", split_axis=0, concat_axis=0, tiled=True)
     other_near_pair = ring(core_other)
-    core_other_near = swap(other_near, "core")
     out = place(
         [
             (near_pair, 0, tp, slot(0, back, 1), 0),
             (core_near, 0, tp, slot(0, -back, 1), 0),
             (core_near_pair, 0, tp, slot(0, -back, 0), 0),
             (other, 0, tp, slot(1, 0, 0), 0),
+            (core_other, 0, tp, slot(1, 0, 1), 0),
             (far, 0, tp, slot(0, 2, 0), 0),
             (core_far, 0, tp, slot(0, 2, 1), 0),
-            (core_other, 0, tp, slot(1, 0, 1), 0),
-            (other_near, 0, tp, slot(1, back, 0), 0),
-            (core_other_near, 0, tp, slot(1, -back, 1), 0),
         ],
         shape,
         out,
     )
-    out, other_near_pair, other_far = lax.optimization_barrier((out, other_near_pair, other_far))
+    other_near, other_near_pair, other_far, out = lax.optimization_barrier((other_near, other_near_pair, other_far, out))
+    core_other_near = swap(other_near, "core")
     core_other_near_pair = swap(other_near_pair, "core")
     core_other_far = swap(other_far, "core")
     attended = terms[0].astype(F32)
-    for peer in range(1, tp):
+    for peer in range(1, 4):
         attended = attended + terms[peer].astype(F32)
     attended = attended.astype(BF16)
     out = place(
         [
+            (other_near, 0, tp, slot(1, back, 0), 0),
+            (core_other_near, 0, tp, slot(1, -back, 1), 0),
             (other_near_pair, 0, tp, slot(1, back, 1), 0),
+            (core_other_near_pair, 0, tp, slot(1, -back, 0), 0),
             (other_far, 0, tp, slot(1, 2, 0), 0),
-            (core_other_near_pair, 0, tp, slot(1, -back, 0), 0),
             (core_other_far, 0, tp, slot(1, 2, 1), 0),
         ],
         shape,
@@ -307,7 +310,7 @@
 
 
 def solution(mesh):
-    fine = jax.sharding.Mesh(mesh.devices.reshape(2, 4, 2, mesh.shape["tp"]), REP + (TP,))
+    fine = jax.sharding.Mesh(mesh.devices.reshape(2, 4, 2, 4, 2), REP + TP)
     in_specs = (
         P(REP, None, None),
         P(),
@@ -318,7 +321,7 @@
         P(REP, None, TP, None),
         P(REP, None, TP, None),
         P(REP),
-        P(REP + (TP,), None),
+        P(REP + TP, None),
     )
     out_specs = (P(REP, None, None), P(None, TP))
     return jax.shard_map(body, mesh=fine, in_specs=in_specs, out_specs=out_specs, check_vma=False)

time: 64.8 us -> 63 us (0.972)
  starting transfers between devices: 33.4 us -> 30.4 us
  waiting for transfers between devices: 7.78 us -> 10.3 us
  local copies, waits for them, and re-layouts: 3.74 us -> 2.72 us
    ppermute x10 -> x11, waiting for transfers between devices: 3.22 us -> 8.35 us  [swap(): return lax.ppermute(array, axis, [(0, 1), (1, 0)])]
    all_to_all x1, waiting for transfers between devices: 2.14 us -> 0.01 us  [body(): lax.all_to_all(partial, 'y', split_axis=0, concat_axis=0, tiled=True)]
    ppermute x5, starting transfers between devices: 9 us -> 7.07 us  [ring(): return lax.ppermute(array, ('x', 'core'), pairs)]
    unnamed x4 -> x2, local copies, waits for them, and re-layouts: 1.81 us -> 0.01 us
    all_to_all x1, starting transfers between devices: 5.06 us -> 4.06 us  [body(): lax.all_to_all(partial, 'y', split_axis=0, concat_axis=0, tiled=True)]
    broadcast_in_dim x0 -> x1, local copies, waits for them, and re-layouts: none -> 0.71 us  [body(): partial = jnp.broadcast_to(partial[None], (4,) + partial.shape)]
    ppermute x10 -> x11, starting transfers between devices: 12.9 us -> 12.9 us  [swap(): return lax.ppermute(array, axis, [(0, 1), (1, 0)])]
  transfers between devices with their start and end apart: 17 -> 18, of which waited for: 4 -> 6; matrix products, arithmetic and copies ran while one was open for 4% -> 5% of each run, Pallas kernels for 21% -> 21%
where the time goes in v4:
time: 63 us; the launch traced here: 62.6 us
  starting transfers between devices  30.4 us (48%)
  Pallas kernels  15.4 us (24%)
  waiting for transfers between devices  10.3 us (16%)
  local copies, waits for them, and re-layouts  2.72 us (4%)
  other arithmetic  2.39 us (4%)
  between operations  1.37 us (2%)
    ppermute x11, starting transfers between devices, swap(): return lax.ppermute(array, axis, [(0, 1), (1, 0)])  12.9 us
    pallas_call x1, Pallas kernels, attention(): pl.pallas_call(attention_kernel, out_shape=jax.ShapeDtypeStruct((STEPS, w...  8.37 us
    ppermute x11, waiting for transfers between devices, swap(): return lax.ppermute(array, axis, [(0, 1), (1, 0)])  8.35 us
    ppermute x5, starting transfers between devices, ring(): return lax.ppermute(array, ('x', 'core'), pairs)  7.07 us
    pallas_call x3, Pallas kernels, place(): pl.pallas_call(kernel, out_shape=jax.ShapeDtypeStruct(shape, BF16), in_sp...  7.01 us
    all_to_all x1, starting transfers between devices, body(): own = lax.all_to_all(blocks, TP, split_axis=0, concat_axis=0, tiled=True)  6.37 us
    all_to_all x1, starting transfers between devices, body(): lax.all_to_all(partial, 'y', split_axis=0, concat_axis=0, tiled=True)  4.06 us
    ppermute x5, waiting for transfers between devices, ring(): return lax.ppermute(array, ('x', 'core'), pairs)  1.93 us
  transfers between devices with their start and end apart: 18, of which 6 were waited for; matrix products, arithmetic and copies ran while one was open for 5% of the time, Pallas kernels for 21%

profile of v4, /device:TPU:1, one launch (start us, length us, event | category | flops | bytes accessed | tf_op | source)
XLA Modules:
  0.0 62.6 jit_solution(12224798454832039318)
XLA Ops:
  0.6 1.8 %copy.17 = bf16[5,8,8,768]{3,2,0,1:T(8,128)(2,1)} copy(bf16[5,8,8,768]{3,2,1,0:T(8,128)(2,1)} %bitcast.32) | data formatting | bytes 983040 | tf_op jit(solution)/shard_map/reshape | solution.py:241
  2.5 6.4 %all-to-all-start = ((bf16[8,40,768]{2,1,0:T(8,128)(2,1)}), bf16[8,40,768]{2,1,0:T(8,128)(2,1)S(1)}, u32[]{:S(2)}, u32[]{:S(2)}) async-start(bf16[8,40,768]{2,1,0:T(8,128)(2,1)} %bitcast.27), calls=%async_computation | async-start | bytes 983040 | tf_op jit(solution)/shard_map/all_to_all | solution.py:242
  9.6 0.7 %pad_maximum_fusion = (f32[4,128]{1,0:T(4,128)}, f32[4,128]{1,0:T(4,128)}) fusion(f32[4,64]{1,0:T(4,128)S(1)} %get-tuple-element.30, f32[4,64]{1,0:T(4,128)S(1)} %get-tuple-element.29, f32[4,64]{1,0:T(4,128)S(1)} %get-tuple-element.28), kind=kLoop, calls=%fused_computation.5 | loop fusion | flops 1024 | bytes 7168 | tf_op jit(solution)/shard_map/concatenate | solution.py:25
  10.3 8.4 %attention.1 = bf16[4,5120]{1,0:T(4,128)(2,1)} custom-call(s32[1]{0:T(128)} %copy.20.length_ref, f32[4,128]{1,0:T(4,128)} %get-tuple-element.31.cos_ref, f32[4,128]{1,0:T(4,128)} %get-tuple-element.32.sin_ref, bf16[4,5120]{1,0:T(4,128)(2,1)} %bitcast.33, bf16[5120]{0:T(1024)(128)(2,1)} %in_gain_hbm.1, bf16[128]{0:T(256)(128)(2,1)} %q_gain_hbm.1, ...), custom_call_target="tpu_custom_call" | custom-call | flops 120000000 | bytes 17400000 | tf_op jit(solution)/shard_map/attention/pallas_call | solution.py:151
  18.7 1.0 %collective-permute-start.1 = (bf16[8,40,768]{2,1,0:T(8,128)(2,1)S(1)}, bf16[8,40,768]{2,1,0:T(8,128)(2,1)S(1)}, u32[]{:S(2)}, u32[]{:S(2)}) collective-permute-start(bf16[8,40,768]{2,1,0:T(8,128)(2,1)S(1)} %all-to-all-done.refs_0_), channel_id=1, source_target_pairs={{0,8},{8,0},{1,9},{9,1},{2,10},{10,2},{3,11},{11,3},{4,12},{12,4},... | collective-permute-start | bytes 1474568 | tf_op jit(solution)/shard_map/ppermute | solution.py:219
  19.7 2.5 %collective-permute-start.3 = (bf16[8,40,768]{2,1,0:T(8,128)(2,1)S(1)}, bf16[8,40,768]{2,1,0:T(8,128)(2,1)S(1)}, u32[]{:S(2)}, u32[]{:S(2)}) collective-permute-start(bf16[8,40,768]{2,1,0:T(8,128)(2,1)S(1)} %all-to-all-done.refs_0_), channel_id=1, source_target_pairs={{0,16},{8,56},{16,32},{24,8},{32,48},{40,24},{48,0},{56,40},{1,17}... | collective-permute-start | bytes 1474568 | tf_op jit(solution)/shard_map/ppermute | solution.py:226
  22.2 3.3 %collective-permute-start = (bf16[8,40,768]{2,1,0:T(8,128)(2,1)S(1)}, bf16[8,40,768]{2,1,0:T(8,128)(2,1)S(1)}, u32[]{:S(2)}, u32[]{:S(2)}) collective-permute-start(bf16[8,40,768]{2,1,0:T(8,128)(2,1)S(1)} %all-to-all-done.refs_0_), channel_id=1, source_target_pairs={{0,64},{64,0},{1,65},{65,1},{2,66},{66,2},{3,67},{67,3},{4,68},{68... | collective-permute-start | bytes 1474568 | tf_op jit(solution)/shard_map/ppermute | solution.py:219
  26.1 1.9 %collective-permute-done.3.refs_2_ = bf16[8,40,768]{2,1,0:T(8,128)(2,1)S(1)} collective-permute-done((bf16[8,40,768]{2,1,0:T(8,128)(2,1)S(1)}, bf16[8,40,768]{2,1,0:T(8,128)(2,1)S(1)}, u32[]{:S(2)}, u32[]{:S(2)}) %collective-permute-start.3) | collective-permute-done | bytes 491552 | tf_op jit(solution)/shard_map/ppermute | solution.py:226
  28.0 1.7 %collective-permute-start.5 = (bf16[4,5120]{1,0:T(4,128)(2,1)}, bf16[4,5120]{1,0:T(4,128)(2,1)S(1)}, u32[]{:S(2)}, u32[]{:S(2)}) collective-permute-start(bf16[4,5120]{1,0:T(4,128)(2,1)} %attention.1), channel_id=1, source_target_pairs={{0,1},{1,0},{2,3},{3,2},{4,5},{5,4},{6,7},{7,6},{8,9},{9,8},{10,11... | collective-permute-start | bytes 122888 | tf_op jit(solution)/shard_map/ppermute | solution.py:219
  29.8 3.3 %collective-permute-start.8 = (bf16[8,40,768]{2,1,0:T(8,128)(2,1)S(1)}, bf16[8,40,768]{2,1,0:T(8,128)(2,1)S(1)}, u32[]{:S(2)}, u32[]{:S(2)}) collective-permute-start(bf16[8,40,768]{2,1,0:T(8,128)(2,1)S(1)} %collective-permute-done.3.refs_2_), channel_id=1, source_target_pairs={{0,16},{8,56},{16,32},{24,8},{32,48},{40,24},{48,0},{56,40},{1,17}... | collective-permute-start | bytes 1474568 | tf_op jit(solution)/shard_map/ppermute | solution.py:226
  33.1 1.7 %place.3.refs_7_ = bf16[16,8,40,768]{3,2,1,0:T(8,128)(2,1)} custom-call(s32[3]{0:T(128)S(1)} %pad_add_fusion.slots_ref, bf16[8,40,768]{2,1,0:T(8,128)(2,1)S(1)} %all-to-all-done.refs_0_, bf16[8,40,768]{2,1,0:T(8,128)(2,1)S(1)} %collective-permute-done.1.refs_1_, bf16[8,40,768]{2,1,0:T(8,128)(2,1)S(1)} %collective-permute-done.3.refs_2_), custom_call_target="tpu_custom_call" | custom-call | bytes 2949120 | tf_op jit(solution)/shard_map/place/pallas_call | solution.py:203
  34.7 1.7 %collective-permute-done.refs_3_ = bf16[8,40,768]{2,1,0:T(8,128)(2,1)S(1)} collective-permute-done((bf16[8,40,768]{2,1,0:T(8,128)(2,1)S(1)}, bf16[8,40,768]{2,1,0:T(8,128)(2,1)S(1)}, u32[]{:S(2)}, u32[]{:S(2)}) %collective-permute-start) | collective-permute-done | bytes 491552 | tf_op jit(solution)/shard_map/ppermute | solution.py:219
  36.5 2.4 %collective-permute-done.5 = bf16[4,5120]{1,0:T(4,128)(2,1)S(1)} collective-permute-done((bf16[4,5120]{1,0:T(4,128)(2,1)}, bf16[4,5120]{1,0:T(4,128)(2,1)S(1)}, u32[]{:S(2)}, u32[]{:S(2)}) %collective-permute-start.5) | collective-permute-done | bytes 40992 | tf_op jit(solution)/shard_map/ppermute | solution.py:219
  38.9 0.7 %collective-permute-start.6 = (bf16[8,40,768]{2,1,0:T(8,128)(2,1)S(1)}, bf16[8,40,768]{2,1,0:T(8,128)(2,1)S(1)}, u32[]{:S(2)}, u32[]{:S(2)}) collective-permute-start(bf16[8,40,768]{2,1,0:T(8,128)(2,1)S(1)} %collective-permute-done.refs_3_), channel_id=1, source_target_pairs={{0,16},{8,56},{16,32},{24,8},{32,48},{40,24},{48,0},{56,40},{1,17}... | collective-permute-start | bytes 1474568 | tf_op jit(solution)/shard_map/ppermute | solution.py:226
  39.6 2.4 %collective-permute-start.12 = (bf16[8,40,768]{2,1,0:T(8,128)(2,1)S(1)}, bf16[8,40,768]{2,1,0:T(8,128)(2,1)}, u32[]{:S(2)}, u32[]{:S(2)}) collective-permute-start(bf16[8,40,768]{2,1,0:T(8,128)(2,1)S(1)} %collective-permute-done.8.refs_5_), channel_id=1, source_target_pairs={{0,8},{8,0},{1,9},{9,1},{2,10},{10,2},{3,11},{11,3},{4,12},{12,4},... | collective-permute-start | bytes 1474568 | tf_op jit(solution)/shard_map/ppermute | solution.py:219
  42.0 3.3 %collective-permute-start.9 = (bf16[8,40,768]{2,1,0:T(8,128)(2,1)S(1)}, bf16[8,40,768]{2,1,0:T(8,128)(2,1)S(1)}, u32[]{:S(2)}, u32[]{:S(2)}) collective-permute-start(bf16[8,40,768]{2,1,0:T(8,128)(2,1)S(1)} %collective-permute-done.8.refs_5_), channel_id=1, source_target_pairs={{0,64},{64,0},{1,65},{65,1},{2,66},{66,2},{3,67},{67,3},{4,68},{68... | collective-permute-start | bytes 1474568 | tf_op jit(solution)/shard_map/ppermute | solution.py:219
  45.3 0.7 %broadcast_in_dim.2 = bf16[4,4,5120]{2,1,0:T(4,128)(2,1)} broadcast(bf16[4,5120]{1,0:T(4,128)(2,1)S(1)} %add_convert_fusion.1), dimensions={1,2} | broadcast | bytes 204800 | tf_op jit(solution)/shard_map/broadcast_in_dim | solution.py:255
  46.1 4.1 %all-to-all-start.1 = ((bf16[4,4,5120]{2,1,0:T(4,128)(2,1)}), bf16[4,4,5120]{2,1,0:T(4,128)(2,1)}, u32[]{:S(2)}, u32[]{:S(2)}) async-start(bf16[4,4,5120]{2,1,0:T(4,128)(2,1)} %broadcast_in_dim.2), calls=%async_computation.1 | async-start | bytes 327680 | tf_op jit(solution)/shard_map/all_to_all | solution.py:274
  50.4 3.2 %place.4.refs_6_ = bf16[16,8,40,768]{3,2,1,0:T(8,128)(2,1)} custom-call(s32[7]{0:T(128)S(1)} %stack.75.slots_ref, bf16[8,40,768]{2,1,0:T(8,128)(2,1)S(1)} %collective-permute-done.2.refs_0_, bf16[8,40,768]{2,1,0:T(8,128)(2,1)S(1)} %collective-permute-done.10.refs_1_, ...), custom_call_target="tpu_custom_call", output_to_operand_aliasing={{}: (8, {})} | custom-call | bytes 6881280 | tf_op jit(solution)/shard_map/place/pallas_call | solution.py:203
  53.5 3.4 %collective-permute-done.9.refs_4_ = bf16[8,40,768]{2,1,0:T(8,128)(2,1)S(1)} collective-permute-done((bf16[8,40,768]{2,1,0:T(8,128)(2,1)S(1)}, bf16[8,40,768]{2,1,0:T(8,128)(2,1)S(1)}, u32[]{:S(2)}, u32[]{:S(2)}) %collective-permute-start.9) | collective-permute-done | bytes 491552 | tf_op jit(solution)/shard_map/ppermute | solution.py:219
  56.9 0.6 collective-permute-start.13
  58.0 1.5 %add_convert_fusion = bf16[1,4,5120]{2,1,0:T(4,128)(2,1)} fusion(bf16[4,4,5120]{2,1,0:T(4,128)(2,1)} %all-to-all-done.1), kind=kLoop, calls=%fused_computation.1 | loop fusion | flops 163840 | bytes 204800 | tf_op jit(solution)/shard_map/convert_element_type | solution.py:296
  59.7 0.7 %collective-permute-done.15.refs_5_ = bf16[8,40,768]{2,1,0:T(8,128)(2,1)S(1)} collective-permute-done((bf16[8,40,768]{2,1,0:T(8,128)(2,1)S(1)}, bf16[8,40,768]{2,1,0:T(8,128)(2,1)S(1)}, u32[]{:S(2)}, u32[]{:S(2)}) %collective-permute-start.15) | collective-permute-done | bytes 491552 | tf_op jit(solution)/shard_map/ppermute | solution.py:219
  60.4 2.2 %place.5 = bf16[16,8,40,768]{3,2,1,0:T(8,128)(2,1)} custom-call(s32[6]{0:T(128)S(1)} %stack.67.slots_ref, bf16[8,40,768]{2,1,0:T(8,128)(2,1)S(1)} %collective-permute-done.6.refs_0_, bf16[8,40,768]{2,1,0:T(8,128)(2,1)S(1)} %collective-permute-done.13.refs_1_, bf16[8,40,768]{2,1,0:T(8,128)(2,1)S(1)} %collective-permute-done.7.refs_2_, ...), custom_call_target="tpu_custom_call", output_to_operand_aliasing={{}: (7, {})} | custom-call | bytes 5898240 | tf_op jit(solution)/shard_map/place/pallas_call | solution.py:203
  (29 shorter events, 1.8 us)
Async XLA Ops:
  2.5 16.2 %all-to-all-start = ((bf16[8,40,768]{2,1,0:T(8,128)(2,1)}), bf16[8,40,768]{2,1,0:T(8,128)(2,1)S(1)}, u32[]{:S(2)}, u32[]{:S(2)}) async-start(bf16[8,40,768]{2,1,0:T(8,128)(2,1)} %bitcast.27), calls=%async_computation | async-start | bytes 983040 | tf_op jit(solution)/shard_map/all_to_all | solution.py:242
  18.7 20.2 %copy-start = (bf16[4,5120]{1,0:T(4,128)(2,1)S(1)}, bf16[4,5120]{1,0:T(4,128)(2,1)}, u32[]{:S(2)}) copy-start(bf16[4,5120]{1,0:T(4,128)(2,1)} %attention.1) | copy-start | bytes 122884
  18.7 6.8 %collective-permute-start.1 = (bf16[8,40,768]{2,1,0:T(8,128)(2,1)S(1)}, bf16[8,40,768]{2,1,0:T(8,128)(2,1)S(1)}, u32[]{:S(2)}, u32[]{:S(2)}) collective-permute-start(bf16[8,40,768]{2,1,0:T(8,128)(2,1)S(1)} %all-to-all-done.refs_0_), channel_id=1, source_target_pairs={{0,8},{8,0},{1,9},{9,1},{2,10},{10,2},{3,11},{11,3},{4,12},{12,4},... | collective-permute-start | bytes 1474568 | tf_op jit(solution)/shard_map/ppermute | solution.py:219
  19.7 8.3 %collective-permute-start.3 = (bf16[8,40,768]{2,1,0:T(8,128)(2,1)S(1)}, bf16[8,40,768]{2,1,0:T(8,128)(2,1)S(1)}, u32[]{:S(2)}, u32[]{:S(2)}) collective-permute-start(bf16[8,40,768]{2,1,0:T(8,128)(2,1)S(1)} %all-to-all-done.refs_0_), channel_id=1, source_target_pairs={{0,16},{8,56},{16,32},{24,8},{32,48},{40,24},{48,0},{56,40},{1,17}... | collective-permute-start | bytes 1474568 | tf_op jit(solution)/shard_map/ppermute | solution.py:226
  22.2 14.3 %collective-permute-start = (bf16[8,40,768]{2,1,0:T(8,128)(2,1)S(1)}, bf16[8,40,768]{2,1,0:T(8,128)(2,1)S(1)}, u32[]{:S(2)}, u32[]{:S(2)}) collective-permute-start(bf16[8,40,768]{2,1,0:T(8,128)(2,1)S(1)} %all-to-all-done.refs_0_), channel_id=1, source_target_pairs={{0,64},{64,0},{1,65},{65,1},{2,66},{66,2},{3,67},{67,3},{4,68},{68... | collective-permute-start | bytes 1474568 | tf_op jit(solution)/shard_map/ppermute | solution.py:219
  25.5 11.0 %collective-permute-start.2 = (bf16[8,40,768]{2,1,0:T(8,128)(2,1)S(1)}, bf16[8,40,768]{2,1,0:T(8,128)(2,1)S(1)}, u32[]{:S(2)}, u32[]{:S(2)}) collective-permute-start(bf16[8,40,768]{2,1,0:T(8,128)(2,1)S(1)} %collective-permute-done.1.refs_1_), channel_id=1, source_target_pairs={{0,16},{8,56},{16,32},{24,8},{32,48},{40,24},{48,0},{56,40},{1,17}... | collective-permute-start | bytes 1474568 | tf_op jit(solution)/shard_map/ppermute | solution.py:226
  28.0 10.9 %collective-permute-start.5 = (bf16[4,5120]{1,0:T(4,128)(2,1)}, bf16[4,5120]{1,0:T(4,128)(2,1)S(1)}, u32[]{:S(2)}, u32[]{:S(2)}) collective-permute-start(bf16[4,5120]{1,0:T(4,128)(2,1)} %attention.1), channel_id=1, source_target_pairs={{0,1},{1,0},{2,3},{3,2},{4,5},{5,4},{6,7},{7,6},{8,9},{9,8},{10,11... | collective-permute-start | bytes 122888 | tf_op jit(solution)/shard_map/ppermute | solution.py:219
  29.8 9.8 %collective-permute-start.8 = (bf16[8,40,768]{2,1,0:T(8,128)(2,1)S(1)}, bf16[8,40,768]{2,1,0:T(8,128)(2,1)S(1)}, u32[]{:S(2)}, u32[]{:S(2)}) collective-permute-start(bf16[8,40,768]{2,1,0:T(8,128)(2,1)S(1)} %collective-permute-done.3.refs_2_), channel_id=1, source_target_pairs={{0,16},{8,56},{16,32},{24,8},{32,48},{40,24},{48,0},{56,40},{1,17}... | collective-permute-start | bytes 1474568 | tf_op jit(solution)/shard_map/ppermute | solution.py:226
  33.1 13.0 %collective-permute-start.10 = (bf16[8,40,768]{2,1,0:T(8,128)(2,1)S(1)}, bf16[8,40,768]{2,1,0:T(8,128)(2,1)S(1)}, u32[]{:S(2)}, u32[]{:S(2)}) collective-permute-start(bf16[8,40,768]{2,1,0:T(8,128)(2,1)S(1)} %collective-permute-done.3.refs_2_), channel_id=1, source_target_pairs={{0,8},{8,0},{1,9},{9,1},{2,10},{10,2},{3,11},{11,3},{4,12},{12,4},... | collective-permute-start | bytes 1474568 | tf_op jit(solution)/shard_map/ppermute | solution.py:219
  36.5 5.5 %collective-permute-start.4 = (bf16[8,40,768]{2,1,0:T(8,128)(2,1)S(1)}, bf16[8,40,768]{2,1,0:T(8,128)(2,1)}, u32[]{:S(2)}, u32[]{:S(2)}) collective-permute-start(bf16[8,40,768]{2,1,0:T(8,128)(2,1)S(1)} %collective-permute-done.refs_3_), channel_id=1, source_target_pairs={{0,8},{8,0},{1,9},{9,1},{2,10},{10,2},{3,11},{11,3},{4,12},{12,4},... | collective-permute-start | bytes 1474568 | tf_op jit(solution)/shard_map/ppermute | solution.py:219
  38.9 14.6 %collective-permute-start.6 = (bf16[8,40,768]{2,1,0:T(8,128)(2,1)S(1)}, bf16[8,40,768]{2,1,0:T(8,128)(2,1)S(1)}, u32[]{:S(2)}, u32[]{:S(2)}) collective-permute-start(bf16[8,40,768]{2,1,0:T(8,128)(2,1)S(1)} %collective-permute-done.refs_3_), channel_id=1, source_target_pairs={{0,16},{8,56},{16,32},{24,8},{32,48},{40,24},{48,0},{56,40},{1,17}... | collective-permute-start | bytes 1474568 | tf_op jit(solution)/shard_map/ppermute | solution.py:226
  39.6 10.8 %collective-permute-start.11 = (bf16[8,40,768]{2,1,0:T(8,128)(2,1)S(1)}, bf16[8,40,768]{2,1,0:T(8,128)(2,1)}, u32[]{:S(2)}, u32[]{:S(2)}) collective-permute-start(bf16[8,40,768]{2,1,0:T(8,128)(2,1)S(1)} %collective-permute-done.2.refs_0_), channel_id=1, source_target_pairs={{0,8},{8,0},{1,9},{9,1},{2,10},{10,2},{3,11},{11,3},{4,12},{12,4},... | collective-permute-start | bytes 1474568 | tf_op jit(solution)/shard_map/ppermute | solution.py:219
  39.6 10.8 %collective-permute-start.12 = (bf16[8,40,768]{2,1,0:T(8,128)(2,1)S(1)}, bf16[8,40,768]{2,1,0:T(8,128)(2,1)}, u32[]{:S(2)}, u32[]{:S(2)}) collective-permute-start(bf16[8,40,768]{2,1,0:T(8,128)(2,1)S(1)} %collective-permute-done.8.refs_5_), channel_id=1, source_target_pairs={{0,8},{8,0},{1,9},{9,1},{2,10},{10,2},{3,11},{11,3},{4,12},{12,4},... | collective-permute-start | bytes 1474568 | tf_op jit(solution)/shard_map/ppermute | solution.py:219
  42.0 14.9 %collective-permute-start.9 = (bf16[8,40,768]{2,1,0:T(8,128)(2,1)S(1)}, bf16[8,40,768]{2,1,0:T(8,128)(2,1)S(1)}, u32[]{:S(2)}, u32[]{:S(2)}) collective-permute-start(bf16[8,40,768]{2,1,0:T(8,128)(2,1)S(1)} %collective-permute-done.8.refs_5_), channel_id=1, source_target_pairs={{0,64},{64,0},{1,65},{65,1},{2,66},{66,2},{3,67},{67,3},{4,68},{68... | collective-permute-start | bytes 1474568 | tf_op jit(solution)/shard_map/ppermute | solution.py:219
  46.0 10.9 %collective-permute-start.7 = (bf16[8,40,768]{2,1,0:T(8,128)(2,1)}, bf16[8,40,768]{2,1,0:T(8,128)(2,1)S(1)}, u32[]{:S(2)}, u32[]{:S(2)}) collective-permute-start(bf16[8,40,768]{2,1,0:T(8,128)(2,1)} %collective-permute-done.4.refs_4_), channel_id=1, source_target_pairs={{0,16},{8,56},{16,32},{24,8},{32,48},{40,24},{48,0},{56,40},{1,17}... | collective-permute-start | bytes 1474568 | tf_op jit(solution)/shard_map/ppermute | solution.py:226
  46.1 11.9 %all-to-all-start.1 = ((bf16[4,4,5120]{2,1,0:T(4,128)(2,1)}), bf16[4,4,5120]{2,1,0:T(4,128)(2,1)}, u32[]{:S(2)}, u32[]{:S(2)}) async-start(bf16[4,4,5120]{2,1,0:T(4,128)(2,1)} %broadcast_in_dim.2), calls=%async_computation.1 | async-start | bytes 327680 | tf_op jit(solution)/shard_map/all_to_all | solution.py:274
  56.9 2.6 %collective-permute-start.13 = (bf16[8,40,768]{2,1,0:T(8,128)(2,1)S(1)}, bf16[8,40,768]{2,1,0:T(8,128)(2,1)S(1)}, u32[]{:S(2)}, u32[]{:S(2)}) collective-permute-start(bf16[8,40,768]{2,1,0:T(8,128)(2,1)S(1)} %collective-permute-done.6.refs_0_), channel_id=1, source_target_pairs={{0,8},{8,0},{1,9},{9,1},{2,10},{10,2},{3,11},{11,3},{4,12},{12,4},... | collective-permute-start | bytes 1474568 | tf_op jit(solution)/shard_map/ppermute | solution.py:219
  57.5 2.2 %collective-permute-start.14 = (bf16[8,40,768]{2,1,0:T(8,128)(2,1)S(1)}, bf16[8,40,768]{2,1,0:T(8,128)(2,1)S(1)}, u32[]{:S(2)}, u32[]{:S(2)}) collective-permute-start(bf16[8,40,768]{2,1,0:T(8,128)(2,1)S(1)} %collective-permute-done.7.refs_2_), channel_id=1, source_target_pairs={{0,8},{8,0},{1,9},{9,1},{2,10},{10,2},{3,11},{11,3},{4,12},{12,4},... | collective-permute-start | bytes 1474568 | tf_op jit(solution)/shard_map/ppermute | solution.py:219
  57.5 2.9 %collective-permute-start.15 = (bf16[8,40,768]{2,1,0:T(8,128)(2,1)S(1)}, bf16[8,40,768]{2,1,0:T(8,128)(2,1)S(1)}, u32[]{:S(2)}, u32[]{:S(2)}) collective-permute-start(bf16[8,40,768]{2,1,0:T(8,128)(2,1)S(1)} %collective-permute-done.9.refs_4_), channel_id=1, source_target_pairs={{0,8},{8,0},{1,9},{9,1},{2,10},{10,2},{3,11},{11,3},{4,12},{12,4},... | collective-permute-start | bytes 1474568 | tf_op jit(solution)/shard_map/ppermute | solution.py:219

commit v5 on v4

--- a/solution.py
+++ b/solution.py
@@ -249,11 +249,11 @@
     other = swap(own, "z_hi")
     core_own = swap(own, "core")
     near = ring(own)
-    near, partial = lax.optimization_barrier((near, partial))
+    near_pair = ring(core_own)
+    near_pair, partial = lax.optimization_barrier((near_pair, partial))
     pair = swap(partial, "z_lo")
     partial = (partial.astype(F32) + pair.astype(F32)).astype(BF16)
     partial = jnp.broadcast_to(partial[None], (4,) + partial.shape)
-    near_pair = ring(core_own)
     out = place(
         [
             (own, 0, tp, slot(0, 0, 0), 0),
@@ -267,7 +267,7 @@
     core_near_pair = swap(near_pair, "core")
     core_far = swap(far, "core")
     other_far = swap(far, "z_hi")
-    other, near_pair, out = lax.optimization_barrier((other, near_pair, out))
+    other, out = lax.optimization_barrier((other, out))
     other_near = ring(other)
     core_other = swap(other, "core")
     core_other, partial = lax.optimization_barrier((core_other, partial))

time: 63 us -> 62.3 us (0.989)
  waiting for transfers between devices: 10.3 us -> 5.05 us
  starting transfers between devices: 30.4 us -> 33.1 us
  local copies, waits for them, and re-layouts: 2.72 us -> 4.57 us
    ppermute x11, waiting for transfers between devices: 8.35 us -> 1.4 us  [swap(): return lax.ppermute(array, axis, [(0, 1), (1, 0)])]
    ppermute x5, starting transfers between devices: 7.07 us -> 10.3 us  [ring(): return lax.ppermute(array, ('x', 'core'), pairs)]
    unnamed x2 -> x6, local copies, waits for them, and re-layouts: 0.01 us -> 1.85 us
    ppermute x5, waiting for transfers between devices: 1.93 us -> 2.84 us  [ring(): return lax.ppermute(array, ('x', 'core'), pairs)]
    ppermute x11, starting transfers between devices: 12.9 us -> 12 us  [swap(): return lax.ppermute(array, axis, [(0, 1), (1, 0)])]
    all_to_all x1, waiting for transfers between devices: 0.01 us -> 0.8 us  [body(): lax.all_to_all(partial, 'y', split_axis=0, concat_axis=0, tiled=True)]
  transfers between devices with their start and end apart: 18 -> 18, of which waited for: 6 -> 5; matrix products, arithmetic and copies ran while one was open for 5% -> 5% of each run, Pallas kernels for 21% -> 21%
where the time goes in v5:
time: 62.3 us; the launch traced here: 61.8 us
  starting transfers between devices  33.1 us (53%)
  Pallas kernels  15.2 us (24%)
  waiting for transfers between devices  5.05 us (8%)
  local copies, waits for them, and re-layouts  4.57 us (7%)
  other arithmetic  2.4 us (4%)
  between operations  1.4 us (2%)
    ppermute x11, starting transfers between devices, swap(): return lax.ppermute(array, axis, [(0, 1), (1, 0)])  12 us
    ppermute x5, starting transfers between devices, ring(): return lax.ppermute(array, ('x', 'core'), pairs)  10.3 us
    pallas_call x1, Pallas kernels, attention(): pl.pallas_call(attention_kernel, out_shape=jax.ShapeDtypeStruct((STEPS, w...  8.39 us
    pallas_call x3, Pallas kernels, place(): pl.pallas_call(kernel, out_shape=jax.ShapeDtypeStruct(shape, BF16), in_sp...  6.85 us
    all_to_all x1, starting transfers between devices, body(): own = lax.all_to_all(blocks, TP, split_axis=0, concat_axis=0, tiled=True)  6.37 us
    all_to_all x1, starting transfers between devices, body(): lax.all_to_all(partial, 'y', split_axis=0, concat_axis=0, tiled=True)  4.4 us
    ppermute x5, waiting for transfers between devices, ring(): return lax.ppermute(array, ('x', 'core'), pairs)  2.84 us
    unnamed x6, local copies, waits for them, and re-layouts  1.85 us
  transfers between devices with their start and end apart: 18, of which 5 were waited for; matrix products, arithmetic and copies ran while one was open for 5% of the time, Pallas kernels for 21%

profile of v5, /device:TPU:1, one launch (start us, length us, event | category | flops | bytes accessed | tf_op | source)
XLA Modules:
  0.0 61.8 jit_solution(9457827613336864567)
XLA Ops:
  0.6 1.8 %copy.17 = bf16[5,8,8,768]{3,2,0,1:T(8,128)(2,1)} copy(bf16[5,8,8,768]{3,2,1,0:T(8,128)(2,1)} %bitcast.32) | data formatting | bytes 983040 | tf_op jit(solution)/shard_map/reshape | solution.py:241
  2.5 6.4 %all-to-all-start = ((bf16[8,40,768]{2,1,0:T(8,128)(2,1)}), bf16[8,40,768]{2,1,0:T(8,128)(2,1)S(1)}, u32[]{:S(2)}, u32[]{:S(2)}) async-start(bf16[8,40,768]{2,1,0:T(8,128)(2,1)} %bitcast.27), calls=%async_computation | async-start | bytes 983040 | tf_op jit(solution)/shard_map/all_to_all | solution.py:242
  10.3 8.4 %attention.1 = bf16[4,5120]{1,0:T(4,128)(2,1)} custom-call(s32[1]{0:T(128)} %copy.20.length_ref, f32[4,128]{1,0:T(4,128)} %get-tuple-element.29.cos_ref, f32[4,128]{1,0:T(4,128)} %get-tuple-element.30.sin_ref, bf16[4,5120]{1,0:T(4,128)(2,1)} %bitcast.33, bf16[5120]{0:T(1024)(128)(2,1)} %in_gain_hbm.1, bf16[128]{0:T(256)(128)(2,1)} %q_gain_hbm.1, ...), custom_call_target="tpu_custom_call" | custom-call | flops 120000000 | bytes 17400000 | tf_op jit(solution)/shard_map/attention/pallas_call | solution.py:151
  18.7 1.0 %collective-permute-start.1 = (bf16[8,40,768]{2,1,0:T(8,128)(2,1)S(1)}, bf16[8,40,768]{2,1,0:T(8,128)(2,1)S(1)}, u32[]{:S(2)}, u32[]{:S(2)}) collective-permute-start(bf16[8,40,768]{2,1,0:T(8,128)(2,1)S(1)} %all-to-all-done.refs_0_), channel_id=1, source_target_pairs={{0,8},{8,0},{1,9},{9,1},{2,10},{10,2},{3,11},{11,3},{4,12},{12,4},... | collective-permute-start | bytes 1474568 | tf_op jit(solution)/shard_map/ppermute | solution.py:219
  19.8 2.5 %collective-permute-start.2 = (bf16[8,40,768]{2,1,0:T(8,128)(2,1)S(1)}, bf16[8,40,768]{2,1,0:T(8,128)(2,1)S(1)}, u32[]{:S(2)}, u32[]{:S(2)}) collective-permute-start(bf16[8,40,768]{2,1,0:T(8,128)(2,1)S(1)} %all-to-all-done.refs_0_), channel_id=1, source_target_pairs={{0,16},{8,56},{16,32},{24,8},{32,48},{40,24},{48,0},{56,40},{1,17}... | collective-permute-start | bytes 1474568 | tf_op jit(solution)/shard_map/ppermute | solution.py:226
  22.2 1.5 %collective-permute-start.4 = (bf16[8,40,768]{2,1,0:T(8,128)(2,1)S(1)}, bf16[8,40,768]{2,1,0:T(8,128)(2,1)S(1)}, u32[]{:S(2)}, u32[]{:S(2)}) collective-permute-start(bf16[8,40,768]{2,1,0:T(8,128)(2,1)S(1)} %collective-permute-done.1.refs_1_), channel_id=1, source_target_pairs={{0,16},{8,56},{16,32},{24,8},{32,48},{40,24},{48,0},{56,40},{1,17}... | collective-permute-start | bytes 1474568 | tf_op jit(solution)/shard_map/ppermute | solution.py:226
  23.7 3.3 %collective-permute-start = (bf16[8,40,768]{2,1,0:T(8,128)(2,1)S(1)}, bf16[8,40,768]{2,1,0:T(8,128)(2,1)S(1)}, u32[]{:S(2)}, u32[]{:S(2)}) collective-permute-start(bf16[8,40,768]{2,1,0:T(8,128)(2,1)S(1)} %all-to-all-done.refs_0_), channel_id=1, source_target_pairs={{0,64},{64,0},{1,65},{65,1},{2,66},{66,2},{3,67},{67,3},{4,68},{68... | collective-permute-start | bytes 1474568 | tf_op jit(solution)/shard_map/ppermute | solution.py:219
  27.0 1.0 %collective-permute-done.2.refs_2_ = bf16[8,40,768]{2,1,0:T(8,128)(2,1)S(1)} collective-permute-done((bf16[8,40,768]{2,1,0:T(8,128)(2,1)S(1)}, bf16[8,40,768]{2,1,0:T(8,128)(2,1)S(1)}, u32[]{:S(2)}, u32[]{:S(2)}) %collective-permute-start.2) | collective-permute-done | bytes 491552 | tf_op jit(solution)/shard_map/ppermute | solution.py:226
  28.0 3.4 %collective-permute-start.8 = (bf16[8,40,768]{2,1,0:T(8,128)(2,1)S(1)}, bf16[8,40,768]{2,1,0:T(8,128)(2,1)S(1)}, u32[]{:S(2)}, u32[]{:S(2)}) collective-permute-start(bf16[8,40,768]{2,1,0:T(8,128)(2,1)S(1)} %collective-permute-done.2.refs_2_), channel_id=1, source_target_pairs={{0,16},{8,56},{16,32},{24,8},{32,48},{40,24},{48,0},{56,40},{1,17}... | collective-permute-start | bytes 1474568 | tf_op jit(solution)/shard_map/ppermute | solution.py:226
  31.4 1.9 %collective-permute-done.4.refs_0_ = bf16[8,40,768]{2,1,0:T(8,128)(2,1)S(1)} collective-permute-done((bf16[8,40,768]{2,1,0:T(8,128)(2,1)S(1)}, bf16[8,40,768]{2,1,0:T(8,128)(2,1)S(1)}, u32[]{:S(2)}, u32[]{:S(2)}) %collective-permute-start.4) | collective-permute-done | bytes 491552 | tf_op jit(solution)/shard_map/ppermute | solution.py:226
  33.3 1.7 %collective-permute-start.5 = (bf16[4,5120]{1,0:T(4,128)(2,1)}, bf16[4,5120]{1,0:T(4,128)(2,1)S(1)}, u32[]{:S(2)}, u32[]{:S(2)}) collective-permute-start(bf16[4,5120]{1,0:T(4,128)(2,1)} %attention.1), channel_id=1, source_target_pairs={{0,1},{1,0},{2,3},{3,2},{4,5},{5,4},{6,7},{7,6},{8,9},{9,8},{10,11... | collective-permute-start | bytes 122888 | tf_op jit(solution)/shard_map/ppermute | solution.py:219
  35.1 1.7 %place.3.refs_7_ = bf16[16,8,40,768]{3,2,1,0:T(8,128)(2,1)} custom-call(s32[3]{0:T(128)S(1)} %pad_add_fusion.slots_ref, bf16[8,40,768]{2,1,0:T(8,128)(2,1)S(1)} %all-to-all-done.refs_0_, bf16[8,40,768]{2,1,0:T(8,128)(2,1)S(1)} %collective-permute-done.1.refs_1_, bf16[8,40,768]{2,1,0:T(8,128)(2,1)S(1)} %collective-permute-done.2.refs_2_), custom_call_target="tpu_custom_call" | custom-call | bytes 2949120 | tf_op jit(solution)/shard_map/place/pallas_call | solution.py:203
  36.8 1.3 %collective-permute-done.refs_3_ = bf16[8,40,768]{2,1,0:T(8,128)(2,1)S(1)} collective-permute-done((bf16[8,40,768]{2,1,0:T(8,128)(2,1)S(1)}, bf16[8,40,768]{2,1,0:T(8,128)(2,1)S(1)}, u32[]{:S(2)}, u32[]{:S(2)}) %collective-permute-start) | collective-permute-done | bytes 491552 | tf_op jit(solution)/shard_map/ppermute | solution.py:219
  38.1 0.9 %collective-permute-start.3 = (bf16[8,40,768]{2,1,0:T(8,128)(2,1)S(1)}, bf16[8,40,768]{2,1,0:T(8,128)(2,1)S(1)}, u32[]{:S(2)}, u32[]{:S(2)}) collective-permute-start(bf16[8,40,768]{2,1,0:T(8,128)(2,1)S(1)} %collective-permute-done.refs_3_), channel_id=1, source_target_pairs={{0,8},{8,0},{1,9},{9,1},{2,10},{10,2},{3,11},{11,3},{4,12},{12,4},... | collective-permute-start | bytes 1474568 | tf_op jit(solution)/shard_map/ppermute | solution.py:219
  39.0 1.3 %collective-permute-start.6 = (bf16[8,40,768]{2,1,0:T(8,128)(2,1)S(1)}, bf16[8,40,768]{2,1,0:T(8,128)(2,1)S(1)}, u32[]{:S(2)}, u32[]{:S(2)}) collective-permute-start(bf16[8,40,768]{2,1,0:T(8,128)(2,1)S(1)} %collective-permute-done.refs_3_), channel_id=1, source_target_pairs={{0,16},{8,56},{16,32},{24,8},{32,48},{40,24},{48,0},{56,40},{1,17}... | collective-permute-start | bytes 1474568 | tf_op jit(solution)/shard_map/ppermute | solution.py:226
  40.9 3.4 %collective-permute-start.9 = (bf16[8,40,768]{2,1,0:T(8,128)(2,1)S(1)}, bf16[8,40,768]{2,1,0:T(8,128)(2,1)S(1)}, u32[]{:S(2)}, u32[]{:S(2)}) collective-permute-start(bf16[8,40,768]{2,1,0:T(8,128)(2,1)S(1)} %collective-permute-done.8.refs_5_), channel_id=1, source_target_pairs={{0,64},{64,0},{1,65},{65,1},{2,66},{66,2},{3,67},{67,3},{4,68},{68... | collective-permute-start | bytes 1474568 | tf_op jit(solution)/shard_map/ppermute | solution.py:219
  45.1 0.8 %copy-done = bf16[8,40,768]{2,1,0:T(8,128)(2,1)} copy-done((bf16[8,40,768]{2,1,0:T(8,128)(2,1)}, bf16[8,40,768]{2,1,0:T(8,128)(2,1)S(1)}, u32[]{:S(2)}) %copy-start) | copy-done | bytes 491544
  45.9 1.6 %collective-permute-start.7 = (bf16[8,40,768]{2,1,0:T(8,128)(2,1)S(1)}, bf16[8,40,768]{2,1,0:T(8,128)(2,1)S(1)}, u32[]{:S(2)}, u32[]{:S(2)}) collective-permute-start(bf16[8,40,768]{2,1,0:T(8,128)(2,1)S(1)} %collective-permute-done.3.refs_4_), channel_id=1, source_target_pairs={{0,16},{8,56},{16,32},{24,8},{32,48},{40,24},{48,0},{56,40},{1,17}... | collective-permute-start | bytes 1474568 | tf_op jit(solution)/shard_map/ppermute | solution.py:226
  47.6 4.4 %all-to-all-start.1 = ((bf16[4,4,5120]{2,1,0:T(4,128)(2,1)}), bf16[4,4,5120]{2,1,0:T(4,128)(2,1)}, u32[]{:S(2)}, u32[]{:S(2)}) async-start(bf16[4,4,5120]{2,1,0:T(4,128)(2,1)} %broadcast_in_dim.2), calls=%async_computation.1 | async-start | bytes 327680 | tf_op jit(solution)/shard_map/all_to_all | solution.py:274
  52.1 1.0 %copy-done.1 = bf16[8,40,768]{2,1,0:T(8,128)(2,1)S(1)} copy-done((bf16[8,40,768]{2,1,0:T(8,128)(2,1)S(1)}, bf16[8,40,768]{2,1,0:T(8,128)(2,1)}, u32[]{:S(2)}) %copy-start.1) | copy-done | bytes 491544
  53.2 3.0 %place.4.refs_6_ = bf16[16,8,40,768]{3,2,1,0:T(8,128)(2,1)} custom-call(s32[7]{0:T(128)S(1)} %stack.75.slots_ref, bf16[8,40,768]{2,1,0:T(8,128)(2,1)S(1)} %collective-permute-done.4.refs_0_, bf16[8,40,768]{2,1,0:T(8,128)(2,1)S(1)} %copy-done.1, bf16[8,40,768]{2,1,0:T(8,128)(2,1)} %collective-permute-done.11.refs_2_, ...), custom_call_target="tpu_custom_call", output_to_operand_aliasing={{}: (8, {})} | custom-call | bytes 6881280 | tf_op jit(solution)/shard_map/place/pallas_call | solution.py:203
  57.2 0.8 %all-to-all-done.1 = bf16[4,4,5120]{2,1,0:T(4,128)(2,1)} async-done(((bf16[4,4,5120]{2,1,0:T(4,128)(2,1)}), bf16[4,4,5120]{2,1,0:T(4,128)(2,1)}, u32[]{:S(2)}, u32[]{:S(2)}) %all-to-all-start.1) | async-done | bytes 163872 | tf_op jit(solution)/shard_map/all_to_all | solution.py:274
  58.0 1.5 %add_convert_fusion = bf16[1,4,5120]{2,1,0:T(4,128)(2,1)} fusion(bf16[4,4,5120]{2,1,0:T(4,128)(2,1)} %all-to-all-done.1), kind=kLoop, calls=%fused_computation.1 | loop fusion | flops 163840 | bytes 204800 | tf_op jit(solution)/shard_map/convert_element_type | solution.py:296
  59.6 2.2 %place.5 = bf16[16,8,40,768]{3,2,1,0:T(8,128)(2,1)} custom-call(s32[6]{0:T(128)S(1)} %stack.67.slots_ref, bf16[8,40,768]{2,1,0:T(8,128)(2,1)S(1)} %collective-permute-done.6.refs_0_, bf16[8,40,768]{2,1,0:T(8,128)(2,1)S(1)} %collective-permute-done.13.refs_1_, bf16[8,40,768]{2,1,0:T(8,128)(2,1)S(1)} %collective-permute-done.7.refs_2_, ...), custom_call_target="tpu_custom_call", output_to_operand_aliasing={{}: (7, {})} | custom-call | bytes 5898240 | tf_op jit(solution)/shard_map/place/pallas_call | solution.py:203
  (33 shorter events, 3.5 us)
Async XLA Ops:
  2.5 16.2 %all-to-all-start = ((bf16[8,40,768]{2,1,0:T(8,128)(2,1)}), bf16[8,40,768]{2,1,0:T(8,128)(2,1)S(1)}, u32[]{:S(2)}, u32[]{:S(2)}) async-start(bf16[8,40,768]{2,1,0:T(8,128)(2,1)} %bitcast.27), calls=%async_computation | async-start | bytes 983040 | tf_op jit(solution)/shard_map/all_to_all | solution.py:242
  18.7 22.2 %copy-start.2 = (bf16[4,5120]{1,0:T(4,128)(2,1)S(1)}, bf16[4,5120]{1,0:T(4,128)(2,1)}, u32[]{:S(2)}) copy-start(bf16[4,5120]{1,0:T(4,128)(2,1)} %attention.1) | copy-start | bytes 122884
  18.7 3.5 %collective-permute-start.1 = (bf16[8,40,768]{2,1,0:T(8,128)(2,1)S(1)}, bf16[8,40,768]{2,1,0:T(8,128)(2,1)S(1)}, u32[]{:S(2)}, u32[]{:S(2)}) collective-permute-start(bf16[8,40,768]{2,1,0:T(8,128)(2,1)S(1)} %all-to-all-done.refs_0_), channel_id=1, source_target_pairs={{0,8},{8,0},{1,9},{9,1},{2,10},{10,2},{3,11},{11,3},{4,12},{12,4},... | collective-permute-start | bytes 1474568 | tf_op jit(solution)/shard_map/ppermute | solution.py:219
  19.8 8.3 %collective-permute-start.2 = (bf16[8,40,768]{2,1,0:T(8,128)(2,1)S(1)}, bf16[8,40,768]{2,1,0:T(8,128)(2,1)S(1)}, u32[]{:S(2)}, u32[]{:S(2)}) collective-permute-start(bf16[8,40,768]{2,1,0:T(8,128)(2,1)S(1)} %all-to-all-done.refs_0_), channel_id=1, source_target_pairs={{0,16},{8,56},{16,32},{24,8},{32,48},{40,24},{48,0},{56,40},{1,17}... | collective-permute-start | bytes 1474568 | tf_op jit(solution)/shard_map/ppermute | solution.py:226
  22.2 11.0 %collective-permute-start.4 = (bf16[8,40,768]{2,1,0:T(8,128)(2,1)S(1)}, bf16[8,40,768]{2,1,0:T(8,128)(2,1)S(1)}, u32[]{:S(2)}, u32[]{:S(2)}) collective-permute-start(bf16[8,40,768]{2,1,0:T(8,128)(2,1)S(1)} %collective-permute-done.1.refs_1_), channel_id=1, source_target_pairs={{0,16},{8,56},{16,32},{24,8},{32,48},{40,24},{48,0},{56,40},{1,17}... | collective-permute-start | bytes 1474568 | tf_op jit(solution)/shard_map/ppermute | solution.py:226
  23.7 14.4 %collective-permute-start = (bf16[8,40,768]{2,1,0:T(8,128)(2,1)S(1)}, bf16[8,40,768]{2,1,0:T(8,128)(2,1)S(1)}, u32[]{:S(2)}, u32[]{:S(2)}) collective-permute-start(bf16[8,40,768]{2,1,0:T(8,128)(2,1)S(1)} %all-to-all-done.refs_0_), channel_id=1, source_target_pairs={{0,64},{64,0},{1,65},{65,1},{2,66},{66,2},{3,67},{67,3},{4,68},{68... | collective-permute-start | bytes 1474568 | tf_op jit(solution)/shard_map/ppermute | solution.py:219
  28.0 12.3 %collective-permute-start.8 = (bf16[8,40,768]{2,1,0:T(8,128)(2,1)S(1)}, bf16[8,40,768]{2,1,0:T(8,128)(2,1)S(1)}, u32[]{:S(2)}, u32[]{:S(2)}) collective-permute-start(bf16[8,40,768]{2,1,0:T(8,128)(2,1)S(1)} %collective-permute-done.2.refs_2_), channel_id=1, source_target_pairs={{0,16},{8,56},{16,32},{24,8},{32,48},{40,24},{48,0},{56,40},{1,17}... | collective-permute-start | bytes 1474568 | tf_op jit(solution)/shard_map/ppermute | solution.py:226
  33.3 7.5 %collective-permute-start.5 = (bf16[4,5120]{1,0:T(4,128)(2,1)}, bf16[4,5120]{1,0:T(4,128)(2,1)S(1)}, u32[]{:S(2)}, u32[]{:S(2)}) collective-permute-start(bf16[4,5120]{1,0:T(4,128)(2,1)} %attention.1), channel_id=1, source_target_pairs={{0,1},{1,0},{2,3},{3,2},{4,5},{5,4},{6,7},{7,6},{8,9},{9,8},{10,11... | collective-permute-start | bytes 122888 | tf_op jit(solution)/shard_map/ppermute | solution.py:219
  38.1 2.9 %collective-permute-start.3 = (bf16[8,40,768]{2,1,0:T(8,128)(2,1)S(1)}, bf16[8,40,768]{2,1,0:T(8,128)(2,1)S(1)}, u32[]{:S(2)}, u32[]{:S(2)}) collective-permute-start(bf16[8,40,768]{2,1,0:T(8,128)(2,1)S(1)} %collective-permute-done.refs_3_), channel_id=1, source_target_pairs={{0,8},{8,0},{1,9},{9,1},{2,10},{10,2},{3,11},{11,3},{4,12},{12,4},... | collective-permute-start | bytes 1474568 | tf_op jit(solution)/shard_map/ppermute | solution.py:219
  39.0 17.2 %collective-permute-start.6 = (bf16[8,40,768]{2,1,0:T(8,128)(2,1)S(1)}, bf16[8,40,768]{2,1,0:T(8,128)(2,1)S(1)}, u32[]{:S(2)}, u32[]{:S(2)}) collective-permute-start(bf16[8,40,768]{2,1,0:T(8,128)(2,1)S(1)} %collective-permute-done.refs_3_), channel_id=1, source_target_pairs={{0,16},{8,56},{16,32},{24,8},{32,48},{40,24},{48,0},{56,40},{1,17}... | collective-permute-start | bytes 1474568 | tf_op jit(solution)/shard_map/ppermute | solution.py:226
  40.3 4.8 %collective-permute-start.10 = (bf16[8,40,768]{2,1,0:T(8,128)(2,1)S(1)}, bf16[8,40,768]{2,1,0:T(8,128)(2,1)S(1)}, u32[]{:S(2)}, u32[]{:S(2)}) collective-permute-start(bf16[8,40,768]{2,1,0:T(8,128)(2,1)S(1)} %collective-permute-done.2.refs_2_), channel_id=1, source_target_pairs={{0,8},{8,0},{1,9},{9,1},{2,10},{10,2},{3,11},{11,3},{4,12},{12,4},... | collective-permute-start | bytes 1474568 | tf_op jit(solution)/shard_map/ppermute | solution.py:219
  40.3 11.8 %collective-permute-start.11 = (bf16[8,40,768]{2,1,0:T(8,128)(2,1)S(1)}, bf16[8,40,768]{2,1,0:T(8,128)(2,1)}, u32[]{:S(2)}, u32[]{:S(2)}) collective-permute-start(bf16[8,40,768]{2,1,0:T(8,128)(2,1)S(1)} %collective-permute-done.4.refs_0_), channel_id=1, source_target_pairs={{0,8},{8,0},{1,9},{9,1},{2,10},{10,2},{3,11},{11,3},{4,12},{12,4},... | collective-permute-start | bytes 1474568 | tf_op jit(solution)/shard_map/ppermute | solution.py:219
  40.8 11.3 %collective-permute-start.12 = (bf16[8,40,768]{2,1,0:T(8,128)(2,1)S(1)}, bf16[8,40,768]{2,1,0:T(8,128)(2,1)}, u32[]{:S(2)}, u32[]{:S(2)}) collective-permute-start(bf16[8,40,768]{2,1,0:T(8,128)(2,1)S(1)} %collective-permute-done.8.refs_5_), channel_id=1, source_target_pairs={{0,8},{8,0},{1,9},{9,1},{2,10},{10,2},{3,11},{11,3},{4,12},{12,4},... | collective-permute-start | bytes 1474568 | tf_op jit(solution)/shard_map/ppermute | solution.py:219
  40.9 15.2 %collective-permute-start.9 = (bf16[8,40,768]{2,1,0:T(8,128)(2,1)S(1)}, bf16[8,40,768]{2,1,0:T(8,128)(2,1)S(1)}, u32[]{:S(2)}, u32[]{:S(2)}) collective-permute-start(bf16[8,40,768]{2,1,0:T(8,128)(2,1)S(1)} %collective-permute-done.8.refs_5_), channel_id=1, source_target_pairs={{0,64},{64,0},{1,65},{65,1},{2,66},{66,2},{3,67},{67,3},{4,68},{68... | collective-permute-start | bytes 1474568 | tf_op jit(solution)/shard_map/ppermute | solution.py:219
  45.1 0.8 %copy-start = (bf16[8,40,768]{2,1,0:T(8,128)(2,1)}, bf16[8,40,768]{2,1,0:T(8,128)(2,1)S(1)}, u32[]{:S(2)}) copy-start(bf16[8,40,768]{2,1,0:T(8,128)(2,1)S(1)} %collective-permute-done.10.refs_1_) | copy-start | bytes 1474564
  45.9 10.3 %collective-permute-start.7 = (bf16[8,40,768]{2,1,0:T(8,128)(2,1)S(1)}, bf16[8,40,768]{2,1,0:T(8,128)(2,1)S(1)}, u32[]{:S(2)}, u32[]{:S(2)}) collective-permute-start(bf16[8,40,768]{2,1,0:T(8,128)(2,1)S(1)} %collective-permute-done.3.refs_4_), channel_id=1, source_target_pairs={{0,16},{8,56},{16,32},{24,8},{32,48},{40,24},{48,0},{56,40},{1,17}... | collective-permute-start | bytes 1474568 | tf_op jit(solution)/shard_map/ppermute | solution.py:226
  47.6 10.4 %all-to-all-start.1 = ((bf16[4,4,5120]{2,1,0:T(4,128)(2,1)}), bf16[4,4,5120]{2,1,0:T(4,128)(2,1)}, u32[]{:S(2)}, u32[]{:S(2)}) async-start(bf16[4,4,5120]{2,1,0:T(4,128)(2,1)} %broadcast_in_dim.2), calls=%async_computation.1 | async-start | bytes 327680 | tf_op jit(solution)/shard_map/all_to_all | solution.py:274
  52.1 1.0 %copy-start.1 = (bf16[8,40,768]{2,1,0:T(8,128)(2,1)S(1)}, bf16[8,40,768]{2,1,0:T(8,128)(2,1)}, u32[]{:S(2)}) copy-start(bf16[8,40,768]{2,1,0:T(8,128)(2,1)} %copy-done) | copy-start | bytes 1474564
  56.2 3.3 %collective-permute-start.13 = (bf16[8,40,768]{2,1,0:T(8,128)(2,1)S(1)}, bf16[8,40,768]{2,1,0:T(8,128)(2,1)S(1)}, u32[]{:S(2)}, u32[]{:S(2)}) collective-permute-start(bf16[8,40,768]{2,1,0:T(8,128)(2,1)S(1)} %collective-permute-done.6.refs_0_), channel_id=1, source_target_pairs={{0,8},{8,0},{1,9},{9,1},{2,10},{10,2},{3,11},{11,3},{4,12},{12,4},... | collective-permute-start | bytes 1474568 | tf_op jit(solution)/shard_map/ppermute | solution.py:219
  56.7 2.8 %collective-permute-start.14 = (bf16[8,40,768]{2,1,0:T(8,128)(2,1)S(1)}, bf16[8,40,768]{2,1,0:T(8,128)(2,1)S(1)}, u32[]{:S(2)}, u32[]{:S(2)}) collective-permute-start(bf16[8,40,768]{2,1,0:T(8,128)(2,1)S(1)} %collective-permute-done.7.refs_2_), channel_id=1, source_target_pairs={{0,8},{8,0},{1,9},{9,1},{2,10},{10,2},{3,11},{11,3},{4,12},{12,4},... | collective-permute-start | bytes 1474568 | tf_op jit(solution)/shard_map/ppermute | solution.py:219
  56.8 2.8 %collective-permute-start.15 = (bf16[8,40,768]{2,1,0:T(8,128)(2,1)S(1)}, bf16[8,40,768]{2,1,0:T(8,128)(2,1)S(1)}, u32[]{:S(2)}, u32[]{:S(2)}) collective-permute-start(bf16[8,40,768]{2,1,0:T(8,128)(2,1)S(1)} %collective-permute-done.9.refs_4_), channel_id=1, source_target_pairs={{0,8},{8,0},{1,9},{9,1},{2,10},{10,2},{3,11},{11,3},{4,12},{12,4},... | collective-permute-start | bytes 1474568 | tf_op jit(solution)/shard_map/ppermute | solution.py:219
